TPU v7x, 512 devices: a whole 4x8x8 slice. The times are simulated.
512 devices in a mesh: gx: 16 (over y, core), gy: 32 (over x, z).
Axes of the slice: x: 4, y: 8, z: 8, core: 2. Of those that a mesh axis runs over, the one named last changes fastest.
Arguments:
- stencil: bfloat16 [32, 128, 2, 64, 448], P('gx', 'gy')
- inverse_blocks: bfloat16 [32, 128, 64, 128], P('gx', 'gy')
- tentative: bfloat16 [32, 128, 8, 128], P('gx', 'gy'), may hold values from -0.75 to 0.75
- aggregate: int32 [32, 128, 2], P('gx', 'gy'), may hold values from 0 to 7
- fine_residual: float32 [32, 128, 128], P('gx', 'gy'), may hold values from -6 to 6
Outputs:
- coarse: float32 [16, 32, 128, 800], P('gx', 'gy')
- restricted: float32 [16, 32, 64], P('gx', 'gy')
Inputs may be any that keep to these rules, and one draw needn't show every extreme that they name: aggregate numbers are local to the element's patch.
All inputs are finite; a program needn't handle non-finite values.
Results may differ from a plain program's by a relative error of at most 0.004.
Values may be sent and summed in bfloat16 or wider, within the bound.
A program may use at most 64 MiB of HBM per device.

v0:
```python
import jax
import jax.numpy as jnp
from jax import lax
from jax.sharding import PartitionSpec as P

AGG = 8


relax_weight = 0.6
SINGLE_FRAME = [(0, 0)]
NEAR_FRAME = [(0, 0), (-1, 0), (1, 0), (0, -1), (0, 1)]
MIDDLE_FRAME = [
    (across, offset)
    for across in range(-2, 3)
    for offset in range(-2, 3)
    if abs(across) + abs(offset) <= 2
]
OUTER_FRAME = [
    (across, offset)
    for across in range(-3, 4)
    for offset in range(-3, 4)
    if abs(across) + abs(offset) <= 3
]
DIRECTIONS = [(0, 0, 0), (-1, 0, 0), (1, 0, 0), (0, -1, 0), (0, 1, 0), (0, 0, -1), (0, 0, 1)]


def shifted(value, axis, steps):
    count = lax.axis_size(axis)
    first, last = (max(0, -steps), min(count, count - steps))
    return lax.ppermute(value, axis, [(source, source + steps) for source in range(first, last)])


def with_halo(cells, sides, width):
    for axis, dim in sides:
        count = lax.axis_size(axis)
        ends = count - 1
        head = lax.slice_in_dim(cells, 0, width, axis=dim)
        tail = lax.slice_in_dim(cells, cells.shape[dim] - width, cells.shape[dim], axis=dim)
        cells = jnp.concatenate(
            [
                lax.ppermute(tail, axis, [(i, (i + 1) % count) for i in range(ends)]),
                cells,
                lax.ppermute(head, axis, [((i + 1) % count, i) for i in range(ends)]),
            ],
            axis=dim,
        )
    return cells


def from_partner(block, axis, distance):
    count = lax.axis_size(axis)
    route = []
    for low in range(count):
        high = low | 1 << distance
        if high != low and high < count:
            route += [(low, high), (high, low)]
    return lax.ppermute(block, axis, route)


def build_seed(tentative, aggregate):
    xcount, ycount, zcount = aggregate.shape
    mode_count = tentative.shape[2]
    block_size = tentative.shape[3] // zcount
    member = aggregate[..., None] == jnp.arange(AGG, dtype=jnp.int32)
    modal_rows = tentative.reshape(xcount, ycount, mode_count, zcount, block_size).transpose(
        0, 1, 3, 4, 2
    )
    seed_rows = jnp.where(
        member[:, :, :, None, :, None],
        modal_rows[:, :, :, :, None, :],
        jnp.zeros((), tentative.dtype),
    )
    return seed_rows.reshape(xcount, ycount, zcount, block_size, AGG * mode_count)


def couple(stencil, extended, inner_frame, outer_frame):
    xcount, ycount, zcount, block_size = stencil.shape[:4]
    column_width = extended.shape[-1] // len(inner_frame)
    xplace = lax.broadcasted_iota(jnp.int32, (xcount, ycount, zcount, 1, 1), 0)
    yplace = lax.broadcasted_iota(jnp.int32, (xcount, ycount, zcount, 1, 1), 1)
    slot_sums = [
        jnp.zeros((xcount, ycount, zcount, block_size, column_width), jnp.float32)
        for target in outer_frame
    ]
    for direction, (step_x, step_y, step_z) in enumerate(DIRECTIONS):
        coupling = stencil[:, :, :, :, direction * block_size : (direction + 1) * block_size]
        nearby = extended[
            1 + step_x : 1 + step_x + xcount,
            1 + step_y : 1 + step_y + ycount,
            1 + step_z : 1 + step_z + zcount,
        ]
        product_term = jnp.einsum(
            "xyzij,xyzjc->xyzic", coupling, nearby, preferred_element_type=jnp.float32
        )
        if step_x != 0 or step_y != 0:
            if step_x == -1:
                crossing = xplace == 0
            elif step_x == 1:
                crossing = xplace == xcount - 1
            elif step_y == -1:
                crossing = yplace == 0
            else:
                crossing = yplace == ycount - 1
            placements = [((0, 0), jnp.logical_not(crossing)), ((step_x, step_y), crossing)]
        else:
            placements = [((0, 0), None)]
        for (move_x, move_y), allowed in placements:
            for position, (from_x, from_y) in enumerate(inner_frame):
                target = outer_frame.index((move_x + from_x, move_y + from_y))
                portion = product_term[..., position * column_width : (position + 1) * column_width]
                if allowed is not None:
                    portion = jnp.where(allowed, portion, jnp.zeros((), jnp.float32))
                slot_sums[target] = slot_sums[target] + portion
    return jnp.concatenate(slot_sums, axis=-1)


def smooth(stencil, inverse_blocks, seed_rows, seed_ext):
    xcount, ycount, zcount, block_size = stencil.shape[:4]
    applied = couple(stencil, seed_ext, SINGLE_FRAME, NEAR_FRAME).astype(jnp.bfloat16)
    inverse = inverse_blocks.reshape(xcount, ycount, block_size, zcount, block_size)
    relaxed = jnp.einsum("xyizj,xyzjc->xyzic", inverse, applied, preferred_element_type=jnp.float32)
    padding = jnp.zeros(seed_rows.shape[:4] + (4 * seed_rows.shape[4],), jnp.float32)
    seeded = jnp.concatenate([seed_rows.astype(jnp.float32), padding], axis=-1)
    return (seeded - relax_weight * relaxed).astype(jnp.bfloat16)


def galerkin(stencil, prolong, prolong_ext, fine_residual):
    coupled = couple(stencil, prolong_ext, NEAR_FRAME, MIDDLE_FRAME).astype(jnp.bfloat16)
    row_count = prolong.shape[0] * prolong.shape[1] * prolong.shape[2] * prolong.shape[3]
    left_rows = prolong.reshape(row_count, -1)
    right_rows = coupled.reshape(row_count, -1)
    contribution = lax.dot_general(
        left_rows, right_rows, (((0,), (0,)), ((), ())), preferred_element_type=jnp.float32
    )
    restrict_terms = lax.dot_general(
        left_rows.astype(jnp.float32),
        fine_residual.reshape(row_count),
        (((0,), (0,)), ((), ())),
        precision=lax.Precision.HIGHEST,
    )
    return (contribution, restrict_terms)


def deepen(array):
    return jnp.pad(array, ((0, 0), (0, 0), (1, 1), (0, 0), (0, 0)))


def along_gx(payload, step):
    return shifted(payload, "gx", step)


def along_gy(payload, step):
    return shifted(payload, "gy", step)


def body(stencil, inverse_blocks, tentative, aggregate, fine_residual):
    xcount, ycount, zcount, block_size = stencil.shape[:4]
    seed_rows = build_seed(tentative, aggregate)
    width = seed_rows.shape[-1]
    seed_flat = with_halo(seed_rows.reshape(xcount, ycount, -1), (("gx", 0), ("gy", 1)), 1)
    seed_ext = deepen(seed_flat.reshape(xcount + 2, ycount + 2, zcount, block_size, width))
    prolong = smooth(stencil, inverse_blocks, seed_rows, seed_ext)
    prolong_flat = with_halo(prolong.reshape(xcount, ycount, -1), (("gx", 0), ("gy", 1)), 1)
    prolong_ext = deepen(
        prolong_flat.reshape(xcount + 2, ycount + 2, zcount, block_size, 5 * width)
    )
    contribution, restrict_terms = galerkin(stencil, prolong, prolong_ext, fine_residual)

    def outgoing(position):
        return (
            contribution[position * width : (position + 1) * width],
            restrict_terms[position * width : (position + 1) * width],
        )

    arrivals = [
        outgoing(0),
        along_gx(outgoing(1), -1),
        along_gx(outgoing(2), 1),
        along_gy(outgoing(3), -1),
        along_gy(outgoing(4), 1),
    ]
    slot_sums = [jnp.zeros((width, width), jnp.float32) for target in OUTER_FRAME]
    restricted = jnp.zeros((width,), jnp.float32)
    for position, (off_x, off_y) in enumerate(NEAR_FRAME):
        arrived_rows, arrived_terms = arrivals[position]
        restricted = restricted + arrived_terms
        for column, (col_x, col_y) in enumerate(MIDDLE_FRAME):
            target = OUTER_FRAME.index((col_x - off_x, col_y - off_y))
            slot_sums[target] = (
                slot_sums[target] + arrived_rows[:, column * width : (column + 1) * width]
            )
    assembled = jnp.concatenate(slot_sums, axis=-1)
    half_width = assembled.shape[1] // 2
    is_even = lax.axis_index("gx") % 2 == 0
    kept = jnp.where(is_even, assembled[:, :half_width], assembled[:, half_width:])
    given = jnp.where(is_even, assembled[:, half_width:], assembled[:, :half_width])
    taken = from_partner(given, "gx", 0)
    coarse = jnp.where(
        is_even, jnp.concatenate([kept, taken], axis=0), jnp.concatenate([taken, kept], axis=0)
    )
    return (coarse.reshape(1, 1, 2 * width, half_width), restricted.reshape(1, 1, width))


def solution(mesh):
    in_specs = (
        P("gx", "gy", None, None, None),
        P("gx", "gy", None, None),
        P("gx", "gy", None, None),
        P("gx", "gy", None),
        P("gx", "gy", None),
    )
    out_specs = (P("gx", "gy", None, None), P("gx", "gy", None))
    return jax.shard_map(body, mesh=mesh, in_specs=in_specs, out_specs=out_specs, check_vma=False)
```

profile of v0, /device:TPU:30, one launch (start us, length us, event | category | flops | bytes accessed | tf_op | source)
XLA Modules:
  0.0 124.9 jit_solution(5687925672304476998)
XLA Ops:
  0.6 0.8 copy.51
  1.5 0.8 reshape.101
  2.6 0.6 copy.56
  3.1 1.3 %slice.488 = bf16[1,4,8192]{2,1,0:T(4,128)(2,1)S(1)} reshape(bf16[1,4,2,64,8,8]{5,4,3,2,1,0:T(8,128)(2,1)S(1)} %copy.56) | data formatting | bytes 131072 | tf_op jit(solution)/shard_map/slice | solution.py:38
  4.4 1.9 %collective-permute-start = (bf16[1,4,8192]{2,1,0:T(4,128)(2,1)S(1)}, bf16[1,4,8192]{2,1,0:T(4,128)(2,1)S(1)}, u32[]{:S(2)}, u32[]{:S(2)}) collective-permute-start(bf16[1,4,8192]{2,1,0:T(4,128)(2,1)S(1)} %slice.488), channel_id=1, source_target_pairs={{0,32},{32,64},{64,96},{96,128},{128,160},{160,192},{192,224},{224... | collective-permute-start | bytes 196616 | tf_op jit(solution)/shard_map/ppermute | solution.py:41
  6.3 0.6 copy.58
  6.9 1.3 %slice.490 = bf16[1,4,8192]{2,1,0:T(4,128)(2,1)S(1)} reshape(bf16[1,4,2,64,8,8]{5,4,3,2,1,0:T(8,128)(2,1)S(1)} %copy.58) | data formatting | bytes 131072 | tf_op jit(solution)/shard_map/slice | solution.py:37
  8.1 3.8 %collective-permute-start.1 = (bf16[1,4,8192]{2,1,0:T(4,128)(2,1)S(1)}, bf16[1,4,8192]{2,1,0:T(4,128)(2,1)S(1)}, u32[]{:S(2)}, u32[]{:S(2)}) collective-permute-start(bf16[1,4,8192]{2,1,0:T(4,128)(2,1)S(1)} %slice.490), channel_id=1, source_target_pairs={{32,0},{64,32},{96,64},{128,96},{160,128},{192,160},{224,192},{256... | collective-permute-start | bytes 196616 | tf_op jit(solution)/shard_map/ppermute | solution.py:43
  11.9 1.2 copy.57
  13.2 2.6 %select_n.213 = bf16[2,4,8192]{2,1,0:T(4,128)(2,1)S(1)} reshape(bf16[2,4,2,64,8,8]{5,4,3,2,1,0:T(8,128)(2,1)S(1)} %copy.57) | data formatting | bytes 262144 | tf_op jit(solution)/shard_map/jit(_where)/select_n | solution.py:68
  16.7 4.3 %collective-permute-start.2 = (bf16[4,1,8192]{2,1,0:T(2,128)(2,1)S(1)}, bf16[4,1,8192]{2,1,0:T(2,128)(2,1)S(1)}, u32[]{:S(2)}, u32[]{:S(2)}) collective-permute-start(bf16[4,1,8192]{2,1,0:T(2,128)(2,1)S(1)} %get-tuple-element.38), channel_id=1, source_target_pairs={{0,1},{1,2},{2,3},{3,4},{4,5},{5,6},{6,7},{7,8},{8,9},{9,10},{10,1... | collective-permute-start | bytes 196616 | tf_op jit(solution)/shard_map/ppermute | solution.py:41
  21.0 8.9 %collective-permute-start.3 = (bf16[4,1,8192]{2,1,0:T(2,128)(2,1)S(1)}, bf16[4,1,8192]{2,1,0:T(2,128)(2,1)S(1)}, u32[]{:S(2)}, u32[]{:S(2)}) collective-permute-start(bf16[4,1,8192]{2,1,0:T(2,128)(2,1)S(1)} %get-tuple-element.39), channel_id=1, source_target_pairs={{1,0},{2,1},{3,2},{4,3},{5,4},{6,5},{7,6},{8,7},{9,8},{10,9},{11,1... | collective-permute-start | bytes 196616 | tf_op jit(solution)/shard_map/ppermute | solution.py:43
  29.8 1.6 %collective-permute-done.2 = bf16[4,1,8192]{2,1,0:T(2,128)(2,1)S(1)} collective-permute-done((bf16[4,1,8192]{2,1,0:T(2,128)(2,1)S(1)}, bf16[4,1,8192]{2,1,0:T(2,128)(2,1)S(1)}, u32[]{:S(2)}, u32[]{:S(2)}) %collective-permute-start.2) | collective-permute-done | bytes 65568 | tf_op jit(solution)/shard_map/ppermute | solution.py:41
  31.5 1.8 %collective-permute-done.3 = bf16[4,1,8192]{2,1,0:T(2,128)(2,1)S(1)} collective-permute-done((bf16[4,1,8192]{2,1,0:T(2,128)(2,1)S(1)}, bf16[4,1,8192]{2,1,0:T(2,128)(2,1)S(1)}, u32[]{:S(2)}, u32[]{:S(2)}) %collective-permute-start.3) | collective-permute-done | bytes 65568 | tf_op jit(solution)/shard_map/ppermute | solution.py:43
  33.7 0.8 reshape.112
  36.7 0.6 concatenate.62
  38.2 2.5 %collective-permute-start.4 = (bf16[1,4,40960]{2,1,0:T(4,128)(2,1)S(1)}, bf16[1,4,40960]{2,1,0:T(4,128)(2,1)S(1)}, u32[]{:S(2)}, u32[]{:S(2)}) collective-permute-start(bf16[1,4,40960]{2,1,0:T(4,128)(2,1)S(1)} %slice.508), channel_id=1, source_target_pairs={{0,32},{32,64},{64,96},{96,128},{128,160},{160,192},{192,224},{224... | collective-permute-start | bytes 983048 | tf_op jit(solution)/shard_map/ppermute | solution.py:41
  41.2 3.2 %collective-permute-start.5 = (bf16[1,4,40960]{2,1,0:T(4,128)(2,1)S(1)}, bf16[1,4,40960]{2,1,0:T(4,128)(2,1)S(1)}, u32[]{:S(2)}, u32[]{:S(2)}) collective-permute-start(bf16[1,4,40960]{2,1,0:T(4,128)(2,1)S(1)} %slice.510), channel_id=1, source_target_pairs={{32,0},{64,32},{96,64},{128,96},{160,128},{192,160},{224,192},{256... | collective-permute-start | bytes 983048 | tf_op jit(solution)/shard_map/ppermute | solution.py:43
  44.5 1.0 reshape.104
  45.5 0.7 copy.68
  47.2 1.7 %collective-permute-done.5 = bf16[1,4,40960]{2,1,0:T(4,128)(2,1)S(1)} collective-permute-done((bf16[1,4,40960]{2,1,0:T(4,128)(2,1)S(1)}, bf16[1,4,40960]{2,1,0:T(4,128)(2,1)S(1)}, u32[]{:S(2)}, u32[]{:S(2)}) %collective-permute-start.5) | collective-permute-done | bytes 327712 | tf_op jit(solution)/shard_map/ppermute | solution.py:43
  49.4 1.1 pad_maximum_fusion.4
  50.5 1.9 %collective-permute-start.6 = (bf16[4,1,40960]{2,0,1:T(4,128)(2,1)S(1)}, bf16[4,1,40960]{2,0,1:T(4,128)(2,1)S(1)}, u32[]{:S(2)}, u32[]{:S(2)}) collective-permute-start(bf16[4,1,40960]{2,0,1:T(4,128)(2,1)S(1)} %get-tuple-element.13), channel_id=1, source_target_pairs={{0,1},{1,2},{2,3},{3,4},{4,5},{5,6},{6,7},{7,8},{8,9},{9,10},{10,1... | collective-permute-start | bytes 983048 | tf_op jit(solution)/shard_map/ppermute | solution.py:41
  52.5 6.5 %collective-permute-start.7 = (bf16[4,1,40960]{2,0,1:T(4,128)(2,1)S(1)}, bf16[4,1,40960]{2,0,1:T(4,128)(2,1)}, u32[]{:S(2)}, u32[]{:S(2)}) collective-permute-start(bf16[4,1,40960]{2,0,1:T(4,128)(2,1)S(1)} %get-tuple-element.14), channel_id=1, source_target_pairs={{1,0},{2,1},{3,2},{4,3},{5,4},{6,5},{7,6},{8,7},{9,8},{10,9},{11,1... | collective-permute-start | bytes 983048 | tf_op jit(solution)/shard_map/ppermute | solution.py:43
  59.4 2.6 %collective-permute-done.6 = bf16[4,1,40960]{2,0,1:T(4,128)(2,1)S(1)} collective-permute-done((bf16[4,1,40960]{2,0,1:T(4,128)(2,1)S(1)}, bf16[4,1,40960]{2,0,1:T(4,128)(2,1)S(1)}, u32[]{:S(2)}, u32[]{:S(2)}) %collective-permute-start.6) | collective-permute-done | bytes 327712 | tf_op jit(solution)/shard_map/ppermute | solution.py:41
  62.1 0.7 copy-done.6
  62.8 0.7 collective-permute-done.7
  63.5 3.8 %pad_maximum_fusion = bf16[4,6,40960]{2,0,1:T(4,128)(2,1)S(1)} fusion(bf16[4,1,40960]{2,0,1:T(4,128)(2,1)} %collective-permute-done.7, bf16[1,4,40960]{2,0,1:T(2,128)(2,1)} %copy-done.2, bf16[2,4,40960]{2,0,1:T(2,128)(2,1)S(1)} %copy.68, bf16[1,4,40960]{2,0,1:T(2,128)(2,1)} %copy-done.1, bf16[4,1,40960]{2,0,1:T(4,128)(2,1)} %copy-done.6), kind=kLoop, calls=%fused_computation | loop fusion | flops 9830400 | bytes 3932160 | tf_op jit(solution)/shard_map/concatenate | solution.py:39
  67.3 4.0 %reshape.105 = bf16[4,6,2,64,320]{4,3,2,0,1:T(8,128)(2,1)} reshape(bf16[4,6,40960]{2,0,1:T(4,128)(2,1)S(1)} %pad_maximum_fusion) | data formatting | bytes 3932160 | tf_op jit(solution)/shard_map/reshape | solution.py:165
  71.3 2.0 %convolution_bitcast_fusion.6 = f32[2,4,2,64,320]{3,4,2,1,0:T(8,128)S(1)} fusion(bf16[4,6,2,64,320]{4,3,2,0,1:T(8,128)(2,1)} %reshape.105, bf16[2,4,2,64,448]{4,3,2,1,0:T(8,128)(2,1)} %param.5), kind=kOutput, calls=%fused_computation.9 | convolution fusion | flops 41943040 | bytes 3932160 | tf_op jit(solution)/shard_map/xyzij,xyzjc->xyzic/dot_general | solution.py:92
  73.7 0.7 convolution_bitcast_fusion.5
  74.9 0.6 convolution_bitcast_fusion.1
  75.5 0.6 convolution_bitcast_fusion.2
  76.1 0.6 convolution_bitcast_fusion.3
  76.7 0.6 convolution_bitcast_fusion.4
  79.1 0.8 fusion.55
  81.6 1.6 %convolution_bitcast_fusion.7 = f32[320,832]{1,0:T(8,128)S(1)} fusion(bf16[2,4,2,64,320]{4,3,2,1,0:T(8,128)(2,1)S(1)} %fusion, bf16[2,4,2,64,832]{3,4,2,1,0:T(8,128)(2,1)S(1)} %fusion.52), kind=kOutput, calls=%fused_computation.12 | convolution fusion | flops 545259520 | bytes 3424256 | tf_op jit(solution)/shard_map/dot_general | solution.py:132
  83.3 5.0 %collective-permute-start.11 = (f32[64,832]{1,0:T(8,128)S(1)}, f32[64,832]{1,0:T(8,128)S(1)}, u32[]{:S(2)}, u32[]{:S(2)}) collective-permute-start(f32[64,832]{1,0:T(8,128)S(1)} %get-tuple-element.23), channel_id=1, source_target_pairs={{32,0},{64,32},{96,64},{128,96},{160,128},{192,160},{224,192},{256... | collective-permute-start | bytes 638984 | tf_op jit(solution)/shard_map/ppermute | solution.py:30
  88.4 2.5 %collective-permute-start.8 = (f32[64,832]{1,0:T(8,128)S(1)}, f32[64,832]{1,0:T(8,128)S(1)}, u32[]{:S(2)}, u32[]{:S(2)}) collective-permute-start(f32[64,832]{1,0:T(8,128)S(1)} %get-tuple-element.26), channel_id=1, source_target_pairs={{0,32},{32,64},{64,96},{96,128},{128,160},{160,192},{192,224},{224... | collective-permute-start | bytes 638984 | tf_op jit(solution)/shard_map/ppermute | solution.py:30
  90.9 2.8 %collective-permute-start.9 = (f32[64,832]{1,0:T(8,128)S(1)}, f32[64,832]{1,0:T(8,128)S(1)}, u32[]{:S(2)}, u32[]{:S(2)}) collective-permute-start(f32[64,832]{1,0:T(8,128)S(1)} %get-tuple-element.25), channel_id=1, source_target_pairs={{0,1},{1,2},{2,3},{3,4},{4,5},{5,6},{6,7},{7,8},{8,9},{9,10},{10,1... | collective-permute-start | bytes 638984 | tf_op jit(solution)/shard_map/ppermute | solution.py:30
  93.7 2.4 %collective-permute-start.13 = (f32[64]{0:T(128)S(1)}, f32[64]{0:T(128)S(1)}, u32[]{:S(2)}, u32[]{:S(2)}) collective-permute-start(f32[64]{0:T(128)S(1)} %get-tuple-element.50), channel_id=1, source_target_pairs={{32,0},{64,32},{96,64},{128,96},{160,128},{192,160},{224,192},{256... | collective-permute-start | bytes 776 | tf_op jit(solution)/shard_map/ppermute | solution.py:30
  96.1 4.1 %collective-permute-start.14 = (f32[64]{0:T(128)S(1)}, f32[64]{0:T(128)S(1)}, u32[]{:S(2)}, u32[]{:S(2)}) collective-permute-start(f32[64]{0:T(128)S(1)} %get-tuple-element.53), channel_id=1, source_target_pairs={{0,32},{32,64},{64,96},{96,128},{128,160},{160,192},{192,224},{224... | collective-permute-start | bytes 776 | tf_op jit(solution)/shard_map/ppermute | solution.py:30
  100.3 5.7 %collective-permute-start.15 = (f32[64]{0:T(128)S(1)}, f32[64]{0:T(128)S(1)}, u32[]{:S(2)}, u32[]{:S(2)}) collective-permute-start(f32[64]{0:T(128)S(1)} %get-tuple-element.52), channel_id=1, source_target_pairs={{1,0},{2,1},{3,2},{4,3},{5,4},{6,5},{7,6},{8,7},{9,8},{10,9},{11,1... | collective-permute-start | bytes 776 | tf_op jit(solution)/shard_map/ppermute | solution.py:30
  106.0 1.9 %collective-permute-start.16 = (f32[64]{0:T(128)S(1)}, f32[64]{0:T(128)S(1)}, u32[]{:S(2)}, u32[]{:S(2)}) collective-permute-start(f32[64]{0:T(128)S(1)} %get-tuple-element.51), channel_id=1, source_target_pairs={{0,1},{1,2},{2,3},{3,4},{4,5},{5,6},{6,7},{7,8},{8,9},{9,10},{10,1... | collective-permute-start | bytes 776 | tf_op jit(solution)/shard_map/ppermute | solution.py:30
  107.9 6.0 %collective-permute-start.10 = (f32[64,832]{1,0:T(8,128)S(1)}, f32[64,832]{1,0:T(8,128)S(1)}, u32[]{:S(2)}, u32[]{:S(2)}) collective-permute-start(f32[64,832]{1,0:T(8,128)S(1)} %get-tuple-element.24), channel_id=1, source_target_pairs={{1,0},{2,1},{3,2},{4,3},{5,4},{6,5},{7,6},{8,7},{9,8},{10,9},{11,1... | collective-permute-start | bytes 638984 | tf_op jit(solution)/shard_map/ppermute | solution.py:30
  114.1 4.4 %collective-permute-done.10 = f32[64,832]{1,0:T(8,128)S(1)} collective-permute-done((f32[64,832]{1,0:T(8,128)S(1)}, f32[64,832]{1,0:T(8,128)S(1)}, u32[]{:S(2)}, u32[]{:S(2)}) %collective-permute-start.10) | collective-permute-done | bytes 213024 | tf_op jit(solution)/shard_map/ppermute | solution.py:30
  119.4 3.5 %collective-permute-start.12 = (f32[64,800]{1,0:T(8,128)S(1)}, f32[64,800]{1,0:T(8,128)S(1)}, u32[]{:S(2)}, u32[]{:S(2)}) collective-permute-start(f32[64,800]{1,0:T(8,128)S(1)} %get-tuple-element.35), channel_id=1, source_target_pairs={{0,32},{32,0},{64,96},{96,64},{128,160},{160,128},{192,224},{224,1... | collective-permute-start | bytes 614408 | tf_op jit(solution)/shard_map/ppermute | solution.py:57
  124.0 0.9 copy.84
  (89 shorter events, 13.7 us)
Async XLA Ops:
  0.6 58.3 %copy-start = (f32[2,4,128]{2,1,0:T(4,128)S(1)}, f32[2,4,128]{2,1,0:T(4,128)}, u32[]{:S(2)}) copy-start(f32[2,4,128]{2,1,0:T(4,128)} %param.9) | copy-start | bytes 12292
  4.4 12.0 %collective-permute-start = (bf16[1,4,8192]{2,1,0:T(4,128)(2,1)S(1)}, bf16[1,4,8192]{2,1,0:T(4,128)(2,1)S(1)}, u32[]{:S(2)}, u32[]{:S(2)}) collective-permute-start(bf16[1,4,8192]{2,1,0:T(4,128)(2,1)S(1)} %slice.488), channel_id=1, source_target_pairs={{0,32},{32,64},{64,96},{96,128},{128,160},{160,192},{192,224},{224... | collective-permute-start | bytes 196616 | tf_op jit(solution)/shard_map/ppermute | solution.py:41
  8.1 8.0 %copy-start.7 = (bf16[2,4,64,128]{3,2,1,0:T(8,128)(2,1)S(1)}, bf16[2,4,64,128]{3,2,1,0:T(8,128)(2,1)}, u32[]{:S(2)}) copy-start(bf16[2,4,64,128]{3,2,1,0:T(8,128)(2,1)} %param.6) | copy-start | bytes 393220
  8.1 8.3 %collective-permute-start.1 = (bf16[1,4,8192]{2,1,0:T(4,128)(2,1)S(1)}, bf16[1,4,8192]{2,1,0:T(4,128)(2,1)S(1)}, u32[]{:S(2)}, u32[]{:S(2)}) collective-permute-start(bf16[1,4,8192]{2,1,0:T(4,128)(2,1)S(1)} %slice.490), channel_id=1, source_target_pairs={{32,0},{64,32},{96,64},{128,96},{160,128},{192,160},{224,192},{256... | collective-permute-start | bytes 196616 | tf_op jit(solution)/shard_map/ppermute | solution.py:43
  15.7 18.8 %copy-start.3 = (bf16[2,4,2,64,448]{4,3,2,1,0:T(8,128)(2,1)S(1)}, bf16[2,4,2,64,448]{4,3,2,1,0:T(8,128)(2,1)}, u32[]{:S(2)}) copy-start(bf16[2,4,2,64,448]{4,3,2,1,0:T(8,128)(2,1)} %param.5) | copy-start | bytes 2752516
  16.7 14.8 %collective-permute-start.2 = (bf16[4,1,8192]{2,1,0:T(2,128)(2,1)S(1)}, bf16[4,1,8192]{2,1,0:T(2,128)(2,1)S(1)}, u32[]{:S(2)}, u32[]{:S(2)}) collective-permute-start(bf16[4,1,8192]{2,1,0:T(2,128)(2,1)S(1)} %get-tuple-element.38), channel_id=1, source_target_pairs={{0,1},{1,2},{2,3},{3,4},{4,5},{5,6},{6,7},{7,8},{8,9},{9,10},{10,1... | collective-permute-start | bytes 196616 | tf_op jit(solution)/shard_map/ppermute | solution.py:41
  21.0 12.3 %collective-permute-start.3 = (bf16[4,1,8192]{2,1,0:T(2,128)(2,1)S(1)}, bf16[4,1,8192]{2,1,0:T(2,128)(2,1)S(1)}, u32[]{:S(2)}, u32[]{:S(2)}) collective-permute-start(bf16[4,1,8192]{2,1,0:T(2,128)(2,1)S(1)} %get-tuple-element.39), channel_id=1, source_target_pairs={{1,0},{2,1},{3,2},{4,3},{5,4},{6,5},{7,6},{8,7},{9,8},{10,9},{11,1... | collective-permute-start | bytes 196616 | tf_op jit(solution)/shard_map/ppermute | solution.py:43
  38.2 8.4 %collective-permute-start.4 = (bf16[1,4,40960]{2,1,0:T(4,128)(2,1)S(1)}, bf16[1,4,40960]{2,1,0:T(4,128)(2,1)S(1)}, u32[]{:S(2)}, u32[]{:S(2)}) collective-permute-start(bf16[1,4,40960]{2,1,0:T(4,128)(2,1)S(1)} %slice.508), channel_id=1, source_target_pairs={{0,32},{32,64},{64,96},{96,128},{128,160},{160,192},{192,224},{224... | collective-permute-start | bytes 983048 | tf_op jit(solution)/shard_map/ppermute | solution.py:41
  41.2 7.6 %collective-permute-start.5 = (bf16[1,4,40960]{2,1,0:T(4,128)(2,1)S(1)}, bf16[1,4,40960]{2,1,0:T(4,128)(2,1)S(1)}, u32[]{:S(2)}, u32[]{:S(2)}) collective-permute-start(bf16[1,4,40960]{2,1,0:T(4,128)(2,1)S(1)} %slice.510), channel_id=1, source_target_pairs={{32,0},{64,32},{96,64},{128,96},{160,128},{192,160},{224,192},{256... | collective-permute-start | bytes 983048 | tf_op jit(solution)/shard_map/ppermute | solution.py:43
  47.1 2.2 %copy-start.1 = (bf16[1,4,40960]{2,0,1:T(2,128)(2,1)}, bf16[1,4,40960]{2,0,1:T(2,128)(2,1)S(1)}, u32[]{:S(2)}) copy-start(bf16[1,4,40960]{2,0,1:T(2,128)(2,1)S(1)} %copy.67) | copy-start | bytes 983044
  49.4 1.1 copy-start.2
  50.5 11.5 %collective-permute-start.6 = (bf16[4,1,40960]{2,0,1:T(4,128)(2,1)S(1)}, bf16[4,1,40960]{2,0,1:T(4,128)(2,1)S(1)}, u32[]{:S(2)}, u32[]{:S(2)}) collective-permute-start(bf16[4,1,40960]{2,0,1:T(4,128)(2,1)S(1)} %get-tuple-element.13), channel_id=1, source_target_pairs={{0,1},{1,2},{2,3},{3,4},{4,5},{5,6},{6,7},{7,8},{8,9},{9,10},{10,1... | collective-permute-start | bytes 983048 | tf_op jit(solution)/shard_map/ppermute | solution.py:41
  52.5 11.1 %collective-permute-start.7 = (bf16[4,1,40960]{2,0,1:T(4,128)(2,1)S(1)}, bf16[4,1,40960]{2,0,1:T(4,128)(2,1)}, u32[]{:S(2)}, u32[]{:S(2)}) collective-permute-start(bf16[4,1,40960]{2,0,1:T(4,128)(2,1)S(1)} %get-tuple-element.14), channel_id=1, source_target_pairs={{1,0},{2,1},{3,2},{4,3},{5,4},{6,5},{7,6},{8,7},{9,8},{10,9},{11,1... | collective-permute-start | bytes 983048 | tf_op jit(solution)/shard_map/ppermute | solution.py:43
  62.1 0.7 copy-start.6
  71.3 2.0 %copy-start.4 = (bf16[2,4,2,64,448]{4,3,2,1,0:T(8,128)(2,1)S(1)}, bf16[2,4,2,64,448]{4,3,2,1,0:T(8,128)(2,1)}, u32[]{:S(2)}) copy-start(bf16[2,4,2,64,448]{4,3,2,1,0:T(8,128)(2,1)} %param.5) | copy-start | bytes 2752516
  71.3 2.3 %copy-start.5 = (bf16[4,6,2,64,320]{4,3,2,0,1:T(8,128)(2,1)S(1)}, bf16[4,6,2,64,320]{4,3,2,0,1:T(8,128)(2,1)}, u32[]{:S(2)}) copy-start(bf16[4,6,2,64,320]{4,3,2,0,1:T(8,128)(2,1)} %reshape.105) | copy-start | bytes 5898244
  83.3 16.9 %collective-permute-start.11 = (f32[64,832]{1,0:T(8,128)S(1)}, f32[64,832]{1,0:T(8,128)S(1)}, u32[]{:S(2)}, u32[]{:S(2)}) collective-permute-start(f32[64,832]{1,0:T(8,128)S(1)} %get-tuple-element.23), channel_id=1, source_target_pairs={{32,0},{64,32},{96,64},{128,96},{160,128},{192,160},{224,192},{256... | collective-permute-start | bytes 638984 | tf_op jit(solution)/shard_map/ppermute | solution.py:30
  88.4 17.6 %collective-permute-start.8 = (f32[64,832]{1,0:T(8,128)S(1)}, f32[64,832]{1,0:T(8,128)S(1)}, u32[]{:S(2)}, u32[]{:S(2)}) collective-permute-start(f32[64,832]{1,0:T(8,128)S(1)} %get-tuple-element.26), channel_id=1, source_target_pairs={{0,32},{32,64},{64,96},{96,128},{128,160},{160,192},{192,224},{224... | collective-permute-start | bytes 638984 | tf_op jit(solution)/shard_map/ppermute | solution.py:30
  90.9 17.0 %collective-permute-start.9 = (f32[64,832]{1,0:T(8,128)S(1)}, f32[64,832]{1,0:T(8,128)S(1)}, u32[]{:S(2)}, u32[]{:S(2)}) collective-permute-start(f32[64,832]{1,0:T(8,128)S(1)} %get-tuple-element.25), channel_id=1, source_target_pairs={{0,1},{1,2},{2,3},{3,4},{4,5},{5,6},{6,7},{7,8},{8,9},{9,10},{10,1... | collective-permute-start | bytes 638984 | tf_op jit(solution)/shard_map/ppermute | solution.py:30
  93.7 29.1 %collective-permute-start.13 = (f32[64]{0:T(128)S(1)}, f32[64]{0:T(128)S(1)}, u32[]{:S(2)}, u32[]{:S(2)}) collective-permute-start(f32[64]{0:T(128)S(1)} %get-tuple-element.50), channel_id=1, source_target_pairs={{32,0},{64,32},{96,64},{128,96},{160,128},{192,160},{224,192},{256... | collective-permute-start | bytes 776 | tf_op jit(solution)/shard_map/ppermute | solution.py:30
  96.1 26.7 %collective-permute-start.14 = (f32[64]{0:T(128)S(1)}, f32[64]{0:T(128)S(1)}, u32[]{:S(2)}, u32[]{:S(2)}) collective-permute-start(f32[64]{0:T(128)S(1)} %get-tuple-element.53), channel_id=1, source_target_pairs={{0,32},{32,64},{64,96},{96,128},{128,160},{160,192},{192,224},{224... | collective-permute-start | bytes 776 | tf_op jit(solution)/shard_map/ppermute | solution.py:30
  100.3 22.6 %collective-permute-start.15 = (f32[64]{0:T(128)S(1)}, f32[64]{0:T(128)S(1)}, u32[]{:S(2)}, u32[]{:S(2)}) collective-permute-start(f32[64]{0:T(128)S(1)} %get-tuple-element.52), channel_id=1, source_target_pairs={{1,0},{2,1},{3,2},{4,3},{5,4},{6,5},{7,6},{8,7},{9,8},{10,9},{11,1... | collective-permute-start | bytes 776 | tf_op jit(solution)/shard_map/ppermute | solution.py:30
  106.0 16.9 %collective-permute-start.16 = (f32[64]{0:T(128)S(1)}, f32[64]{0:T(128)S(1)}, u32[]{:S(2)}, u32[]{:S(2)}) collective-permute-start(f32[64]{0:T(128)S(1)} %get-tuple-element.51), channel_id=1, source_target_pairs={{0,1},{1,2},{2,3},{3,4},{4,5},{5,6},{6,7},{7,8},{8,9},{9,10},{10,1... | collective-permute-start | bytes 776 | tf_op jit(solution)/shard_map/ppermute | solution.py:30
  107.9 10.5 %collective-permute-start.10 = (f32[64,832]{1,0:T(8,128)S(1)}, f32[64,832]{1,0:T(8,128)S(1)}, u32[]{:S(2)}, u32[]{:S(2)}) collective-permute-start(f32[64,832]{1,0:T(8,128)S(1)} %get-tuple-element.24), channel_id=1, source_target_pairs={{1,0},{2,1},{3,2},{4,3},{5,4},{6,5},{7,6},{8,7},{9,8},{10,9},{11,1... | collective-permute-start | bytes 638984 | tf_op jit(solution)/shard_map/ppermute | solution.py:30
  119.4 4.6 %collective-permute-start.12 = (f32[64,800]{1,0:T(8,128)S(1)}, f32[64,800]{1,0:T(8,128)S(1)}, u32[]{:S(2)}, u32[]{:S(2)}) collective-permute-start(f32[64,800]{1,0:T(8,128)S(1)} %get-tuple-element.35), channel_id=1, source_target_pairs={{0,32},{32,0},{64,96},{96,64},{128,160},{160,128},{192,224},{224,1... | collective-permute-start | bytes 614408 | tf_op jit(solution)/shard_map/ppermute | solution.py:57
where the time goes:
time: 126 us; the launch traced here: 125 us
  starting transfers between devices  66.9 us (53%)
  local copies, waits for them, and re-layouts  21.3 us (17%)
  waiting for transfers between devices  13.9 us (11%)
  other arithmetic  11.6 us (9%)
  matrix products  9.78 us (8%)
  between operations  1.38 us (1%)
    ppermute x8, starting transfers between devices, shifted(): lax.ppermute(value, axis, [(source, source + steps) for source in range(f...  30.5 us
    ppermute x4, starting transfers between devices, with_halo(): lax.ppermute(head, axis, [((i + 1) % count, i) for i in range(ends)])  22.4 us
    ppermute x4, starting transfers between devices, with_halo(): lax.ppermute(tail, axis, [(i, (i + 1) % count) for i in range(ends)])  10.6 us
    dot_general x14, matrix products, couple(): jnp.einsum('xyzij,xyzjc->xyzic', coupling, nearby, preferred_element_type...  7.38 us
    ppermute x4, waiting for transfers between devices, with_halo(): lax.ppermute(tail, axis, [(i, (i + 1) % count) for i in range(ends)])  4.7 us
    ppermute x8, waiting for transfers between devices, shifted(): lax.ppermute(value, axis, [(source, source + steps) for source in range(f...  4.42 us
    ppermute x4, waiting for transfers between devices, with_halo(): lax.ppermute(head, axis, [((i + 1) % count, i) for i in range(ends)])  4.24 us
    concatenate x2, other arithmetic, with_halo(): jnp.concatenate([lax.ppermute(tail, axis, [(i, (i + 1) % count) for i in...  4.22 us
  transfers between devices with their start and end apart: 17, of which 8 were waited for; matrix products, arithmetic and copies ran while one was open for 9% of the time, Pallas kernels for 0%

commit v1 on v0

v1 whole, which is shorter than its diff:
```python
import jax
import jax.numpy as jnp
from jax import lax
from jax.experimental import pallas as pl
from jax.experimental.pallas import tpu as pltpu
from jax.sharding import PartitionSpec as P

MESH = pl.DeviceIdType.MESH
F32, BF16 = jnp.float32, jnp.bfloat16
AGG = 8
MODES = 8
RELAX = 0.6


X_AT, Y_AT = (0, 2, 3, 4), {0: 1, 3: 5}


def nt(left, right):
    return lax.dot_general(left, right, (((1,), (1,)), ((), ())), preferred_element_type=F32)


def expand(tile):
    values, code = tile[0:MODES].astype(F32), tile[MODES : 2 * MODES].astype(F32)
    rows = [jnp.where(code == float(a), values, 0.0) for a in range(AGG)]
    return jnp.concatenate(rows, axis=0).astype(BF16)


def swap(tile):
    return pltpu.roll(tile, 64, 1)


def kernel(
    n_gx,
    n_gy,
    stencil,
    inverse,
    tentative,
    aggregate,
    residual,
    out,
    restricted,
    sten_v,
    inv_v,
    tent_v,
    agg_v,
    res_v,
    w_v,
    wb_v,
    pack_v,
    hx_v,
    hy_v,
    p0_v,
    hp0x_v,
    hp0y_v,
    pc_v,
    hpcx_v,
    hpcy_v,
    st_v,
    lx_v,
    acc_v,
    snd_v,
    rcv_v,
    load_sem,
    send_sem,
    recv_sem,
):
    gx, gy = lax.axis_index("gx"), lax.axis_index("gy")
    odd = lax.rem(gx, 2)
    is_odd = odd == 1
    turn = 2 * odd - 1
    partner = gx - turn
    outer = lax.rem(gx + turn + n_gx, n_gx)
    outer2 = lax.rem(gx + 2 * turn + n_gx, n_gx)
    back2 = lax.rem(gx - 2 * turn + n_gx, n_gx)
    below = lax.rem(gy - 1 + n_gy, n_gy)
    above = lax.rem(gy + 1, n_gy)
    has_outer = jnp.logical_and(gx > 0, gx < n_gx - 1)
    has_below, has_above = gy > 0, gy < n_gy - 1

    loads = []

    def load(src, dst):
        copy = pltpu.make_async_copy(src, dst, load_sem.at[len(loads)])
        copy.start()
        loads.append(copy)
        return copy

    small = []
    for side in range(2):
        x = side + odd - 2 * side * odd
        small.append(load(tentative.at[x], tent_v.at[side]))
        small.append(load(aggregate.at[x], agg_v.at[side]))
    big = []
    for side in range(2):
        x = side + odd - 2 * side * odd
        big.append(load(stencil.at[x], sten_v.at[side]))
        big.append(load(inverse.at[x], inv_v.at[side]))
        big.append(load(residual.at[x], res_v.at[side]))

    barrier = pltpu.get_barrier_semaphore()
    peers = [
        (partner, gy),
        (outer, gy),
        (outer2, gy),
        (back2, gy),
        (gx, below),
        (gx, above),
        (partner, below),
        (partner, above),
    ]
    for peer in peers:
        pl.semaphore_signal(barrier, inc=1, device_id=peer, device_id_type=MESH)

    sends = []

    def send(src, dst, peer):
        at = len(sends)
        copy = pltpu.make_async_remote_copy(
            src_ref=src,
            dst_ref=dst,
            send_sem=send_sem.at[at],
            recv_sem=recv_sem.at[at],
            device_id=peer,
            device_id_type=MESH,
        )
        copy.start()
        sends.append(copy)
        return copy

    lane = lax.broadcasted_iota(jnp.int32, (8, 128), 1)
    for copy in small:
        copy.wait()
    for side in range(2):
        for y in range(4):
            code = jnp.where(
                lane < 64,
                jnp.broadcast_to(agg_v[side, y : y + 1, 0:1], (8, 128)),
                jnp.broadcast_to(agg_v[side, y : y + 1, 1:2], (8, 128)),
            )
            tile = jnp.concatenate([tent_v[side, y].astype(F32), code.astype(F32)], axis=0)
            pack_v[side, y] = tile.astype(BF16)

    pl.semaphore_wait(barrier, len(peers))
    seed_x = [
        send(pack_v.at[0], hx_v.at[0], (outer, gy)),
        send(pack_v.at[1], hx_v.at[1], (partner, gy)),
    ]
    seed_y = [
        send(pack_v.at[:, 0], hy_v.at[1], (gx, below)),
        send(pack_v.at[:, 3], hy_v.at[0], (gx, above)),
    ]

    for y in range(4):
        both = jnp.concatenate([pack_v[0, y], pack_v[1, y]], axis=1)
        st_v[y] = expand(both)

    for copy in big:
        copy.wait()
    wide = lax.broadcasted_iota(jnp.int32, (64, 128), 1)
    low = wide < 64
    zero = jnp.zeros((64, 128), F32)

    def put(kind, y, place, first, second):
        rows = pl.ds(place * 64, 64)
        w_v[y, kind, rows, 0:128] = first.astype(BF16)
        w_v[y, kind, rows, 128:256] = second.astype(BF16)

    for y in range(4):
        for side in range(2):
            inv = inv_v[side, y].astype(F32)
            for z in range(2):
                place = 2 * side + z
                block = jnp.where(low if z == 0 else jnp.logical_not(low), inv, 0.0)
                tiles = [block, zero] if side == 0 else [zero, block]
                wb_v[y, pl.ds(place * 64, 64), 0:128] = tiles[0].astype(BF16)
                wb_v[y, pl.ds(place * 64, 64), 128:256] = tiles[1].astype(BF16)

                a = sten_v[side, y, z, :, 0:128].astype(F32)
                b = sten_v[side, y, z, :, 128:256].astype(F32)
                c = sten_v[side, y, z, :, 256:384].astype(F32)
                d = sten_v[side, y, z, :, 384:448].astype(F32)
                d = jnp.concatenate([d, d], axis=1)
                ra, rb, rc = swap(a), swap(b), swap(c)
                if z == 0:
                    own = jnp.where(low, a, d)
                    toward_o, toward_i = jnp.where(is_odd, b, ra), jnp.where(is_odd, ra, b)
                    toward_m, toward_p = rb, c
                    keep = low
                else:
                    own = jnp.where(low, rc, ra)
                    toward_o, toward_i = jnp.where(is_odd, rb, a), jnp.where(is_odd, a, rb)
                    toward_m, toward_p = b, rc
                    keep = jnp.logical_not(low)
                toward_o = jnp.where(keep, toward_o, 0.0)
                toward_i = jnp.where(keep, toward_i, 0.0)
                toward_m = jnp.where(keep, toward_m, 0.0)
                toward_p = jnp.where(keep, toward_p, 0.0)
                if y == 0:
                    toward_m = jnp.where(has_below, toward_m, 0.0)
                if y == 3:
                    toward_p = jnp.where(has_above, toward_p, 0.0)
                if side == 0:
                    put(0, y, place, own, toward_i)
                    put(1, y, place, jnp.where(has_outer, toward_o, 0.0), zero)
                    put(2, y, place, toward_m, zero)
                    put(3, y, place, toward_p, zero)
                else:
                    put(0, y, place, toward_o, own)
                    put(1, y, place, zero, toward_i)
                    put(2, y, place, zero, toward_m)
                    put(3, y, place, zero, toward_p)

    def first_slot(y):
        applied = nt(st_v[y], w_v[y, 0])
        if y > 0:
            applied = applied + nt(st_v[y - 1], w_v[y, 2])
        if y < 3:
            applied = applied + nt(st_v[y + 1], w_v[y, 3])
        relaxed = nt(applied.astype(BF16), wb_v[y])
        p0_v[y] = (st_v[y].astype(F32) - RELAX * relaxed).astype(BF16)

    first_slot(0)
    first_y = [send(p0_v.at[0], hp0y_v.at[1], (gx, below))]
    first_slot(3)
    first_y.append(send(p0_v.at[3], hp0y_v.at[0], (gx, above)))
    first_slot(1)
    first_slot(2)
    first_x = [
        send(p0_v.at[:, :, 0:128], hp0x_v.at[:, :, 0:128], (outer, gy)),
        send(p0_v.at[:, :, 128:256], hp0x_v.at[:, :, 128:256], (partner, gy)),
    ]

    for copy in seed_x + seed_y:
        copy.wait_recv()

    def side_slots(y):
        halo = jnp.concatenate([hx_v[0, y], hx_v[1, y]], axis=1)
        halos, applied = [halo], [nt(halo, w_v[y, 1]).astype(BF16)]
        if y in (0, 3):
            end = 0 if y == 0 else 1
            halo = jnp.concatenate([hy_v[end, 0], hy_v[end, 1]], axis=1)
            halos.append(halo)
            applied.append(nt(halo, w_v[y, 2 + end]).astype(BF16))
        applied = applied[0] if len(applied) == 1 else jnp.concatenate(applied, axis=0)
        relaxed = nt(applied, wb_v[y])
        for n, at in enumerate([X_AT[y]] + ([Y_AT[y]] if y in Y_AT else [])):
            values = -RELAX * relaxed[16 * n : 16 * n + MODES]
            tile = jnp.concatenate([values, halos[n][MODES:].astype(F32)], axis=0)
            pc_v[at] = tile.astype(BF16)

    side_slots(0)
    side_slots(3)
    side_y = [
        send(pc_v.at[0:2], hpcy_v.at[1], (gx, below)),
        send(pc_v.at[4:6], hpcy_v.at[0], (gx, above)),
    ]
    side_slots(1)
    side_slots(2)
    side_x = [
        send(pc_v.at[:, :, 0:128], hpcx_v.at[:, :, 0:128], (outer, gy)),
        send(pc_v.at[:, :, 128:256], hpcx_v.at[:, :, 128:256], (partner, gy)),
    ]

    out[...] = jnp.zeros(out.shape, F32)
    blank = jnp.zeros((64, 128), BF16)
    for y in range(4):
        full = expand(pc_v[X_AT[y]])
        lx_v[y, 0:64, 0:128] = full[:, 0:128]
        lx_v[y, 0:64, 128:256] = blank
        lx_v[y, 64:128, 0:128] = blank
        lx_v[y, 64:128, 128:256] = full[:, 128:256]
        if y in Y_AT:
            lx_v[y, 128:192] = expand(pc_v[Y_AT[y]])

    def left(y, rows):
        return jnp.concatenate([p0_v[y], lx_v[y, 0 : rows - 64]], axis=0)

    terms = [jnp.zeros((64, 1), F32) for slot in range(5)]
    for y in range(4):
        res = jnp.concatenate([res_v[0, y : y + 1, :], res_v[1, y : y + 1, :]], axis=1)
        blocks = [(0, p0_v[y]), (1, lx_v[y, 0:64]), (2, lx_v[y, 64:128])]
        if y in Y_AT:
            blocks.append((3 if y == 0 else 4, lx_v[y, 128:192]))
        for slot, block in blocks:
            terms[slot] = terms[slot] + jnp.sum(block.astype(F32) * res, axis=1, keepdims=True)

    for y in range(4):
        size = 256 if y in Y_AT else 192
        acc_v[y, 0:size] = nt(left(y, size), w_v[y, 0])
        if y not in Y_AT:
            acc_v[y, 192:256] = jnp.zeros((64, 256), F32)
        if y > 0:
            size = 256 if y - 1 in Y_AT else 192
            acc_v[y, 0:size] = acc_v[y, 0:size] + nt(left(y - 1, size), w_v[y, 2])
        if y < 3:
            size = 256 if y + 1 in Y_AT else 192
            acc_v[y, 0:size] = acc_v[y, 0:size] + nt(left(y + 1, size), w_v[y, 3])

    for copy in first_x + first_y:
        copy.wait_recv()
    for y in range(4):
        part = nt(hp0x_v[y], w_v[y, 1])
        acc_v[y, 64:128, 0:128] = acc_v[y, 64:128, 0:128] + part[:, 0:128]
        acc_v[y, 128:192, 128:256] = acc_v[y, 128:192, 128:256] + part[:, 128:256]
        if y in Y_AT:
            end = 0 if y == 0 else 1
            acc_v[y, 192:256] = acc_v[y, 192:256] + nt(hp0y_v[end], w_v[y, 2 + end])

    for copy in side_y + side_x:
        copy.wait_recv()

    def finish(y):
        if y in Y_AT:
            end = 0 if y == 0 else 1
            fromx = jnp.concatenate([expand(hpcx_v[X_AT[y]]), expand(hpcx_v[Y_AT[y]])], axis=0)
            partx = nt(fromx, w_v[y, 1])
            fromy = jnp.concatenate([expand(hpcy_v[end, 0]), expand(hpcy_v[end, 1])], axis=0)
            party = nt(fromy, w_v[y, 2 + end])
            own = (acc_v[y, 0:64] + partx[0:64] + party[64:128]).astype(BF16)
            corner = (partx[64:128] + party[0:64]).astype(BF16)
            mid = acc_v[y, 64:256].astype(BF16)
            corner_o = jnp.concatenate([corner[:, 0:128], blank], axis=1)
            corner_i = jnp.concatenate([blank, corner[:, 128:256]], axis=1)
            right = jnp.concatenate(
                [own, mid[128:192], corner_o, mid[0:64], corner_i, mid[64:128]], axis=0
            )
            return nt(left(y, 256), right)
        partx = nt(expand(hpcx_v[X_AT[y]]), w_v[y, 1])
        own = (acc_v[y, 0:64] + partx).astype(BF16)
        mid = acc_v[y, 64:256].astype(BF16)
        right = jnp.concatenate([own, mid[128:192], mid[64:128], mid[0:64]], axis=0)
        return nt(left(y, 192), right)

    def pick(first, second):
        return jnp.where(low, first, second)

    def half(tile, near):
        moved = jnp.where(low, tile, pltpu.roll(tile, 96, 1))
        return jnp.where(is_odd, moved, tile) if near else jnp.where(is_odd, tile, moved)

    def with_terms(tile, term):
        upper = term.astype(BF16).astype(F32)
        return jnp.where(wide == 96, upper, jnp.where(wide == 97, term - upper, tile))

    def tiles(product, slot):
        rows = product[slot * 64 : slot * 64 + 64]
        return [rows[:, 128 * t : 128 * t + 128] for t in range(rows.shape[1] // 128)]

    def post(at, values):
        for n, value in enumerate(values):
            snd_v[at + n] = value.astype(BF16)

    g0 = finish(0)
    t0, t1, t2 = tiles(g0, 3)
    post(8, [with_terms(half(pick(jnp.where(is_odd, t0, 0.0), t0), True), terms[3]), t1])
    post(10, [half(pick(jnp.where(is_odd, 0.0, t0), t0), False), t2])
    msgs = [
        send(snd_v.at[8:10], rcv_v.at[8:10], (gx, below)),
        send(snd_v.at[10:12], rcv_v.at[10:12], (partner, below)),
    ]
    g3 = finish(3)
    t0, t1, t2 = tiles(g3, 3)
    post(12, [with_terms(half(pick(jnp.where(is_odd, 0.0, t0), t0), True), terms[4]), t1])
    post(14, [half(pick(jnp.where(is_odd, t0, 0.0), t0), False), t2])
    msgs += [
        send(snd_v.at[12:14], rcv_v.at[12:14], (gx, above)),
        send(snd_v.at[14:16], rcv_v.at[14:16], (partner, above)),
    ]
    g1 = finish(1)
    g2 = finish(2)

    def summed(slot):
        a0, a1, a2 = tiles(g0, slot)
        b0, b1, b2 = tiles(g3, slot)
        c0, c1 = tiles(g1, slot)
        d0, d1 = tiles(g2, slot)
        um, up = a0 + c0, b0 + d0
        mid = c1 + d1
        return um, up, um + up, a1, b1, a1 + b1 + mid, a2, b2, a2 + b2 + swap(mid)

    def by_side(first, second):
        return jnp.where(is_odd, second, first)

    um, up, mid, om, op, o_sum, im, ip, i_sum = summed(1)
    post(
        4,
        [
            with_terms(half(pick(by_side(op, om), o_sum), False), terms[1]),
            pick(mid, up),
            pick(swap(um), i_sum),
        ],
    )
    post(7, [half(pick(by_side(om, op), o_sum), True)])
    msgs += [
        send(snd_v.at[4:7], rcv_v.at[4:7], (outer, gy)),
        send(snd_v.at[7:8], rcv_v.at[7:8], (outer2, gy)),
    ]
    um, up, mid, om, op, o_sum, im, ip, i_sum = summed(2)
    post(3, [with_terms(half(pick(by_side(ip, im), i_sum), False), terms[2])])
    far_a = half(pick(by_side(im, ip), i_sum), True)
    far_b = pick(mid, up)
    far_c = pick(swap(um), o_sum)
    um, up, mid, om, op, o_sum, im, ip, i_sum = summed(0)
    post(
        0,
        [
            half(swap(pick(mid, by_side(up, um))), False),
            swap(pick(ip, i_sum)),
            pick(im, 0.0),
        ],
    )
    msgs += [send(snd_v.at[0:4], rcv_v.at[0:4], (partner, gy))]
    own_a = with_terms(half(swap(pick(mid, by_side(um, up))), True), terms[0])
    own_b = swap(pick(op, o_sum))
    own_c = pick(om, 0.0)

    for copy in msgs:
        copy.wait_recv()

    def got(at):
        return rcv_v[at].astype(F32)

    y_near, y_far = got(13), got(15)
    own_a = own_a + got(3) + got(4) + got(8) + got(12)
    own_b = own_b + got(5) + got(9) + pick(y_near, 0.0)
    own_c = own_c + got(6) + pick(swap(y_near), 0.0)
    far_a = far_a + got(0) + got(7) + got(10) + got(14)
    far_b = far_b + got(1) + got(11) + pick(y_far, 0.0)
    far_c = far_c + got(2) + pick(swap(y_far), 0.0)

    @pl.when(odd == 0)
    def _():
        for row, (a, b, c) in enumerate([(own_a, own_b, own_c), (far_a, far_b, far_c)]):
            rows = pl.ds(row * 64, 64)
            ra, rc = swap(a), swap(c)
            out[0, 0, rows, 128:256] = pick(rc, 0.0)
            out[0, 0, rows, 256:384] = pick(0.0, rc)
            out[0, 0, rows, 384:512] = b
            out[0, 0, rows, 640:768] = pick(0.0, ra)
            out[0, 0, rows, 768:800] = ra[:, 0:32]

    @pl.when(odd == 1)
    def _():
        for row, (a, b, c) in enumerate([(far_a, far_b, far_c), (own_a, own_b, own_c)]):
            rows = pl.ds(row * 64, 64)
            ra, ta = swap(a), pltpu.roll(a, 32, 1)
            tb, tc = pltpu.roll(b, 96, 1), pltpu.roll(c, 32, 1)
            out[0, 0, rows, 0:128] = jnp.where(wide < 32, ra, jnp.where(wide < 96, ta, 0.0))
            out[0, 0, rows, 256:384] = jnp.where(
                wide < 32, 0.0, jnp.where(wide < 96, tc, tb)
            )
            out[0, 0, rows, 384:512] = jnp.where(wide < 96, tb, 0.0)
            out[0, 0, rows, 512:640] = jnp.where(wide < 96, 0.0, tc)
            out[0, 0, rows, 640:768] = jnp.where(wide < 32, tc, 0.0)

    turned = own_a.T
    restricted[0] = turned[96:97, :] + turned[97:98, :]

    for copy in sends:
        copy.wait_send()


def body(stencil, inverse, tentative, aggregate, residual):
    any_space = pl.BlockSpec(memory_space=pl.ANY)
    vmem = pl.BlockSpec(memory_space=pltpu.VMEM)
    scratch = [
        pltpu.VMEM(stencil.shape, BF16),
        pltpu.VMEM(inverse.shape, BF16),
        pltpu.VMEM(tentative.shape, BF16),
        pltpu.VMEM(aggregate.shape, jnp.int32),
        pltpu.VMEM(residual.shape, F32),
        pltpu.VMEM((4, 4, 256, 256), BF16),
        pltpu.VMEM((4, 256, 256), BF16),
        pltpu.VMEM((2, 4, 16, 128), BF16),
        pltpu.VMEM((2, 4, 16, 128), BF16),
        pltpu.VMEM((2, 2, 16, 128), BF16),
        pltpu.VMEM((4, 64, 256), BF16),
        pltpu.VMEM((4, 64, 256), BF16),
        pltpu.VMEM((2, 64, 256), BF16),
        pltpu.VMEM((6, 16, 256), BF16),
        pltpu.VMEM((6, 16, 256), BF16),
        pltpu.VMEM((2, 2, 16, 256), BF16),
        pltpu.VMEM((4, 64, 256), BF16),
        pltpu.VMEM((4, 192, 256), BF16),
        pltpu.VMEM((4, 256, 256), F32),
        pltpu.VMEM((16, 64, 128), BF16),
        pltpu.VMEM((16, 64, 128), BF16),
        pltpu.SemaphoreType.DMA((10,)),
        pltpu.SemaphoreType.DMA((19,)),
        pltpu.SemaphoreType.DMA((19,)),
    ]
    sizes = (lax.axis_size("gx"), lax.axis_size("gy"))

    def call(*refs):
        kernel(*sizes, *refs)

    return pl.pallas_call(
        call,
        out_shape=(
            jax.ShapeDtypeStruct((1, 1, 128, 800), F32),
            jax.ShapeDtypeStruct((1, 1, 64), F32),
        ),
        in_specs=[any_space] * 5,
        out_specs=(vmem, vmem),
        scratch_shapes=scratch,
        compiler_params=pltpu.CompilerParams(
            collective_id=0, has_side_effects=True, vmem_limit_bytes=32 << 20
        ),
        name="galerkin",
    )(stencil, inverse, tentative, aggregate, residual)


def solution(mesh):
    in_specs = (
        P("gx", "gy", None, None, None),
        P("gx", "gy", None, None),
        P("gx", "gy", None, None),
        P("gx", "gy", None),
        P("gx", "gy", None),
    )
    out_specs = (P("gx", "gy", None, None), P("gx", "gy", None))
    return jax.shard_map(body, mesh=mesh, in_specs=in_specs, out_specs=out_specs, check_vma=False)
```

time: 126 us -> 36 us (0.29)
  the two profiles are of different devices: /device:TPU:30 before, /device:TPU:1 now
where the time goes in v1:
time: 36 us; the launch traced here: 35.7 us
  Pallas kernels  30 us (83%)
  local copies, waits for them, and re-layouts  5.07 us (14%)
  between operations  0.65 us (2%)
    pallas_call x1, Pallas kernels, body(): pl.pallas_call(call, out_shape=(jax.ShapeDtypeStruct((1, 1, 128, 800), F3...  30 us
    unnamed x10, local copies, waits for them, and re-layouts  4.14 us
    pallas_call x1, local copies, waits for them, and re-layouts, body(): pl.pallas_call(call, out_shape=(jax.ShapeDtypeStruct((1, 1, 128, 800), F3...  0.93 us

profile of v1, /device:TPU:1, one launch (start us, length us, event | category | flops | bytes accessed | tf_op | source)
XLA Modules:
  0.0 35.7 jit_solution(3762688209864474208)
XLA Ops:
  0.6 0.0 copy-start.3
  0.6 0.8 %copy.7.refs_3_ = s32[2,4,2]{2,1,0:T(4,128)S(1)} copy(s32[2,4,2]{1,2,0:T(2,128)} %param.8) | data formatting | bytes 128 | tf_op args[3]
  1.4 0.0 copy-done.3
  1.4 0.0 copy-start
  1.4 1.2 %copy-done = bf16[2,4,2,64,448]{4,3,2,1,0:T(8,128)(2,1)S(1)} copy-done((bf16[2,4,2,64,448]{4,3,2,1,0:T(8,128)(2,1)S(1)}, bf16[2,4,2,64,448]{4,3,2,1,0:T(8,128)(2,1)}, u32[]{:S(2)}) %copy-start) | copy-done | bytes 917528
  2.6 0.0 copy-start.1
  2.6 0.9 %copy-done.1 = bf16[2,4,64,128]{3,2,1,0:T(8,128)(2,1)S(1)} copy-done((bf16[2,4,64,128]{3,2,1,0:T(8,128)(2,1)S(1)}, bf16[2,4,64,128]{3,2,1,0:T(8,128)(2,1)}, u32[]{:S(2)}) %copy-start.1) | copy-done | bytes 131096
  3.6 0.0 copy-start.2
  3.6 0.7 %copy-done.2 = bf16[2,4,8,128]{3,2,1,0:T(8,128)(2,1)S(1)} copy-done((bf16[2,4,8,128]{3,2,1,0:T(8,128)(2,1)S(1)}, bf16[2,4,8,128]{3,2,1,0:T(8,128)(2,1)}, u32[]{:S(2)}) %copy-start.2) | copy-done | bytes 16408
  4.3 30.0 %galerkin.1 = (f32[1,1,128,800]{3,2,1,0:T(8,128)S(1)}, f32[1,1,64]{2,1,0:T(1,128)S(1)}) custom-call(bf16[2,4,2,64,448]{4,3,2,1,0:T(8,128)(2,1)S(1)} %copy-done, bf16[2,4,64,128]{3,2,1,0:T(8,128)(2,1)S(1)} %copy-done.1, bf16[2,4,8,128]{3,2,1,0:T(8,128)(2,1)S(1)} %copy-done.2, s32[2,4,2]{2,1,0:T(4,128)S(1)} %copy.7.refs_3_, f32[2,4,128]{2,1,0:T(4,128)S(1)} %copy-done.3), custom_call_target="tpu_custom_call" | custom-call | tf_op jit(solution)/shard_map/galerkin/pallas_call | solution.py:497
  34.3 0.9 %copy.8 = f32[1,1,128,800]{2,3,1,0:T(8,128)} copy(f32[1,1,128,800]{3,2,1,0:T(8,128)S(1)} %get-tuple-element.2) | data formatting | bytes 819200 | tf_op jit(solution)/shard_map/galerkin/pallas_call | solution.py:497
  35.2 0.5 %copy.10 = f32[1,1,64]{2,1,0:T(1,128)} copy(f32[1,1,64]{2,1,0:T(1,128)S(1)} %get-tuple-element.7) | data formatting | bytes 512
Async XLA Ops:
  0.6 0.8 %copy-start.3 = (f32[2,4,128]{2,1,0:T(4,128)S(1)}, f32[2,4,128]{2,1,0:T(4,128)}, u32[]{:S(2)}) copy-start(f32[2,4,128]{2,1,0:T(4,128)} %refs_4_.1) | copy-start | bytes 12292
  1.4 1.2 %copy-start = (bf16[2,4,2,64,448]{4,3,2,1,0:T(8,128)(2,1)S(1)}, bf16[2,4,2,64,448]{4,3,2,1,0:T(8,128)(2,1)}, u32[]{:S(2)}) copy-start(bf16[2,4,2,64,448]{4,3,2,1,0:T(8,128)(2,1)} %refs_0_.1) | copy-start | bytes 2752516
  2.6 0.9 %copy-start.1 = (bf16[2,4,64,128]{3,2,1,0:T(8,128)(2,1)S(1)}, bf16[2,4,64,128]{3,2,1,0:T(8,128)(2,1)}, u32[]{:S(2)}) copy-start(bf16[2,4,64,128]{3,2,1,0:T(8,128)(2,1)} %refs_1_.1) | copy-start | bytes 393220
  3.6 0.7 %copy-start.2 = (bf16[2,4,8,128]{3,2,1,0:T(8,128)(2,1)S(1)}, bf16[2,4,8,128]{3,2,1,0:T(8,128)(2,1)}, u32[]{:S(2)}) copy-start(bf16[2,4,8,128]{3,2,1,0:T(8,128)(2,1)} %refs_2_.1) | copy-start | bytes 49156

commit v2 on v1

--- a/solution.py
+++ b/solution.py
@@ -38,7 +38,6 @@
     aggregate,
     residual,
     out,
-    restricted,
     sten_v,
     inv_v,
     tent_v,
@@ -134,8 +133,8 @@
         for y in range(4):
             code = jnp.where(
                 lane < 64,
-                jnp.broadcast_to(agg_v[side, y : y + 1, 0:1], (8, 128)),
-                jnp.broadcast_to(agg_v[side, y : y + 1, 1:2], (8, 128)),
+                jnp.broadcast_to(agg_v[side, 0:1, y : y + 1], (8, 128)),
+                jnp.broadcast_to(agg_v[side, 1:2, y : y + 1], (8, 128)),
             )
             tile = jnp.concatenate([tent_v[side, y].astype(F32), code.astype(F32)], axis=0)
             pack_v[side, y] = tile.astype(BF16)
@@ -428,40 +427,50 @@
     far_b = far_b + got(1) + got(11) + pick(y_far, 0.0)
     far_c = far_c + got(2) + pick(swap(y_far), 0.0)
 
+    def both(own, far):
+        first, second = jnp.where(is_odd, far, own), jnp.where(is_odd, own, far)
+        return jnp.concatenate([first, second], axis=0).T
+
+    a, b, c = both(own_a, far_a), both(own_b, far_b), both(own_c, far_c)
+
     @pl.when(odd == 0)
     def _():
-        for row, (a, b, c) in enumerate([(own_a, own_b, own_c), (far_a, far_b, far_c)]):
-            rows = pl.ds(row * 64, 64)
-            ra, rc = swap(a), swap(c)
-            out[0, 0, rows, 128:256] = pick(rc, 0.0)
-            out[0, 0, rows, 256:384] = pick(0.0, rc)
-            out[0, 0, rows, 384:512] = b
-            out[0, 0, rows, 640:768] = pick(0.0, ra)
-            out[0, 0, rows, 768:800] = ra[:, 0:32]
+        out[128:192] = c[64:128]
+        out[320:384] = c[0:64]
+        out[384:512] = b
+        out[704:800] = a[0:96]
+        out[800:801] = a[96:97] + a[97:98]
 
     @pl.when(odd == 1)
     def _():
-        for row, (a, b, c) in enumerate([(far_a, far_b, far_c), (own_a, own_b, own_c)]):
-            rows = pl.ds(row * 64, 64)
-            ra, ta = swap(a), pltpu.roll(a, 32, 1)
-            tb, tc = pltpu.roll(b, 96, 1), pltpu.roll(c, 32, 1)
-            out[0, 0, rows, 0:128] = jnp.where(wide < 32, ra, jnp.where(wide < 96, ta, 0.0))
-            out[0, 0, rows, 256:384] = jnp.where(
-                wide < 32, 0.0, jnp.where(wide < 96, tc, tb)
-            )
-            out[0, 0, rows, 384:512] = jnp.where(wide < 96, tb, 0.0)
-            out[0, 0, rows, 512:640] = jnp.where(wide < 96, 0.0, tc)
-            out[0, 0, rows, 640:768] = jnp.where(wide < 32, tc, 0.0)
-
-    turned = own_a.T
-    restricted[0] = turned[96:97, :] + turned[97:98, :]
+        out[0:32] = a[64:96]
+        out[32:96] = a[0:64]
+        out[288:352] = c[0:64]
+        out[352:480] = b
+        out[608:672] = c[64:128]
+        out[800:801] = swap(a[96:97] + a[97:98])
 
     for copy in sends:
         copy.wait_send()
 
 
+def finish_kernel(data, coarse, restricted, row, sem):
+    first = pltpu.make_async_copy(data.at[pl.ds(0, 800)], coarse.at[0, 0], sem.at[0])
+    first.start()
+    row[...] = data[800:801, 0:64]
+    second = pltpu.make_async_copy(row, restricted.at[0], sem.at[1])
+    second.start()
+    first.wait()
+    second.wait()
+
+
 def body(stencil, inverse, tentative, aggregate, residual):
-    any_space = pl.BlockSpec(memory_space=pl.ANY)
+    hbm = pl.BlockSpec(memory_space=pltpu.HBM)
+    aggregate = aggregate.transpose(0, 2, 1)
+    operands = [
+        pltpu.with_memory_space_constraint(operand, pltpu.HBM)
+        for operand in (stencil, inverse, tentative, aggregate, residual)
+    ]
     vmem = pl.BlockSpec(memory_space=pltpu.VMEM)
     scratch = [
         pltpu.VMEM(stencil.shape, BF16),
@@ -494,20 +503,29 @@
     def call(*refs):
         kernel(*sizes, *refs)
 
-    return pl.pallas_call(
+    coarse = pl.pallas_call(
         call,
-        out_shape=(
-            jax.ShapeDtypeStruct((1, 1, 128, 800), F32),
-            jax.ShapeDtypeStruct((1, 1, 64), F32),
-        ),
-        in_specs=[any_space] * 5,
-        out_specs=(vmem, vmem),
+        out_shape=pltpu.VMEM((808, 128), F32),
+        in_specs=[hbm] * 5,
+        out_specs=vmem,
         scratch_shapes=scratch,
         compiler_params=pltpu.CompilerParams(
             collective_id=0, has_side_effects=True, vmem_limit_bytes=32 << 20
         ),
         name="galerkin",
-    )(stencil, inverse, tentative, aggregate, residual)
+    )(*operands)
+    coarse, restricted = pl.pallas_call(
+        finish_kernel,
+        out_shape=(
+            jax.ShapeDtypeStruct((1, 1, 800, 128), F32),
+            jax.ShapeDtypeStruct((1, 1, 64), F32),
+        ),
+        in_specs=[pl.BlockSpec(memory_space=pltpu.VMEM)],
+        out_specs=(pl.BlockSpec(memory_space=pl.ANY), pl.BlockSpec(memory_space=pl.ANY)),
+        scratch_shapes=[pltpu.VMEM((1, 64), F32), pltpu.SemaphoreType.DMA((2,))],
+        name="store",
+    )(pltpu.with_memory_space_constraint(coarse, pltpu.VMEM))
+    return coarse.swapaxes(2, 3), restricted
 
 
 def solution(mesh):

time: 36 us -> 31.2 us (0.87)
  local copies, waits for them, and re-layouts: 5.07 us -> 0 us
  Pallas kernels: 30 us -> 30.4 us
    unnamed x10 -> x0, local copies, waits for them, and re-layouts: 4.14 us -> none
    pallas_call x1 -> x0, local copies, waits for them, and re-layouts: 0.93 us -> none  [body(): pl.pallas_call(call, out_shape=(jax.ShapeDtypeStruct((1, 1, 128, 800), F3...]
    pallas_call x1 -> x2, Pallas kernels: 30 us -> 30.4 us  [the longest x1 29.6 us: body(): pl.pallas_call(call, out_shape=pltpu.VMEM((808, 128), F32), in_specs=[hbm...]
where the time goes in v2:
time: 31.2 us; the launch traced here: 31 us
  Pallas kernels  30.4 us (97%)
  between operations  0.64 us (2%)
    pallas_call x1, Pallas kernels, body(): pl.pallas_call(call, out_shape=pltpu.VMEM((808, 128), F32), in_specs=[hbm...  29.6 us
    pallas_call x1, Pallas kernels, body(): pl.pallas_call(finish_kernel, out_shape=(jax.ShapeDtypeStruct((1, 1, 800,...  0.77 us

profile of v2, /device:TPU:1, one launch (start us, length us, event | category | flops | bytes accessed | tf_op | source)
XLA Modules:
  0.0 31.0 jit_solution(6904748432360123132)
XLA Ops:
  0.6 29.6 %galerkin.1.data = f32[808,128]{1,0:T(8,128)S(1)} custom-call(bf16[2,4,2,64,448]{4,3,2,1,0:T(8,128)(2,1)} %refs_0_.1, bf16[2,4,64,128]{3,2,1,0:T(8,128)(2,1)} %refs_1_.1, bf16[2,4,8,128]{3,2,1,0:T(8,128)(2,1)} %refs_2_.1, s32[2,2,4]{2,1,0:T(2,128)} %bitcast.2, f32[2,4,128]{2,1,0:T(4,128)} %refs_4_.1), custom_call_target="tpu_custom_call" | custom-call | tf_op jit(solution)/shard_map/galerkin/pallas_call | solution.py:506
  30.3 0.8 %store.1 = (f32[1,1,800,128]{3,2,1,0:T(8,128)}, f32[1,1,64]{2,1,0:T(1,128)}) custom-call(f32[808,128]{1,0:T(8,128)S(1)} %galerkin.1.data), custom_call_target="tpu_custom_call" | custom-call | tf_op jit(solution)/shard_map/store/pallas_call | solution.py:517

commit v3 on v2

--- a/solution.py
+++ b/solution.py
@@ -45,9 +45,10 @@
     res_v,
     w_v,
     wb_v,
-    pack_v,
-    hx_v,
-    hy_v,
+    hxt_v,
+    hxa_v,
+    hyt_v,
+    hya_v,
     p0_v,
     hp0x_v,
     hp0y_v,
@@ -59,6 +60,8 @@
     acc_v,
     snd_v,
     rcv_v,
+    sny_v,
+    rcy_v,
     load_sem,
     send_sem,
     recv_sem,
@@ -74,7 +77,36 @@
     below = lax.rem(gy - 1 + n_gy, n_gy)
     above = lax.rem(gy + 1, n_gy)
     has_outer = jnp.logical_and(gx > 0, gx < n_gx - 1)
+    has_back = jnp.logical_and(partner > 0, partner < n_gx - 1)
     has_below, has_above = gy > 0, gy < n_gy - 1
+
+    def only(condition, action):
+        if condition is None:
+            action()
+        else:
+            pl.when(condition)(action)
+
+    barrier = pltpu.get_barrier_semaphore()
+    peers = [
+        ((gx, above), has_above),
+        ((partner, above), has_above),
+        ((gx, below), has_below),
+        ((partner, below), has_below),
+        ((outer, gy), has_outer),
+        ((outer2, gy), has_outer),
+        ((back2, gy), has_back),
+        ((partner, gy), None),
+    ]
+    for peer, condition in peers:
+        only(
+            condition,
+            lambda peer=peer: pl.semaphore_signal(
+                barrier, inc=1, device_id=peer, device_id_type=MESH
+            ),
+        )
+    awaited = 1
+    for _, condition in peers[:-1]:
+        awaited = awaited + jnp.where(condition, 1, 0)
 
     loads = []
 
@@ -96,23 +128,9 @@
         big.append(load(inverse.at[x], inv_v.at[side]))
         big.append(load(residual.at[x], res_v.at[side]))
 
-    barrier = pltpu.get_barrier_semaphore()
-    peers = [
-        (partner, gy),
-        (outer, gy),
-        (outer2, gy),
-        (back2, gy),
-        (gx, below),
-        (gx, above),
-        (partner, below),
-        (partner, above),
-    ]
-    for peer in peers:
-        pl.semaphore_signal(barrier, inc=1, device_id=peer, device_id_type=MESH)
-
     sends = []
 
-    def send(src, dst, peer):
+    def send(src, dst, peer, leaves=None, arrives=None):
         at = len(sends)
         copy = pltpu.make_async_remote_copy(
             src_ref=src,
@@ -122,36 +140,69 @@
             device_id=peer,
             device_id_type=MESH,
         )
-        copy.start()
-        sends.append(copy)
-        return copy
+        only(leaves, copy.start)
+        sends.append((copy, leaves))
+        return copy, arrives
+
+    def await_all(copies):
+        for copy, arrives in copies:
+            only(arrives, copy.wait_recv)
+
+    to_outer, to_outer2 = (has_outer, has_outer), (has_outer, has_back)
+    to_below, to_above = (has_below, has_above), (has_above, has_below)
+
+    pl.semaphore_wait(barrier, awaited)
+    x_of = [odd, 1 - odd]
+    seeds = [
+        send(tentative.at[:, 3], hyt_v.at[0], (gx, above), *to_above),
+        send(aggregate, hya_v.at[0], (gx, above), *to_above),
+        send(tentative.at[:, 0], hyt_v.at[1], (gx, below), *to_below),
+        send(aggregate, hya_v.at[1], (gx, below), *to_below),
+        send(tentative.at[x_of[0]], hxt_v.at[0], (outer, gy), *to_outer),
+        send(aggregate.at[x_of[0]], hxa_v.at[0], (outer, gy), *to_outer),
+        send(tentative.at[x_of[1]], hxt_v.at[1], (partner, gy)),
+        send(aggregate.at[x_of[1]], hxa_v.at[1], (partner, gy)),
+    ]
+
+    @pl.when(jnp.logical_not(has_outer))
+    def _():
+        hxt_v[0] = jnp.zeros(hxt_v.shape[1:], BF16)
+        hxa_v[0] = jnp.zeros(hxa_v.shape[1:], jnp.int32)
+        hp0x_v[:, :, 0:128] = jnp.zeros((4, 64, 128), BF16)
+        hpcx_v[:, :, 0:128] = jnp.zeros((6, 16, 128), BF16)
+        rcv_v[4:7] = jnp.zeros((3, 64, 128), BF16)
+
+    @pl.when(jnp.logical_not(has_back))
+    def _():
+        rcv_v[7] = jnp.zeros((64, 128), BF16)
+
+    for end, condition in enumerate((has_below, has_above)):
+
+        @pl.when(jnp.logical_not(condition))
+        def _(end=end):
+            hyt_v[end] = jnp.zeros(hyt_v.shape[1:], BF16)
+            hya_v[end] = jnp.zeros(hya_v.shape[1:], jnp.int32)
+            hp0y_v[end] = jnp.zeros((64, 256), BF16)
+            hpcy_v[end] = jnp.zeros((2, 16, 256), BF16)
+            rcy_v[end] = jnp.zeros((4, 32, 128), BF16)
 
     lane = lax.broadcasted_iota(jnp.int32, (8, 128), 1)
+    def packed(modes, code_0, code_1):
+        code = jnp.where(
+            lane < 64, jnp.broadcast_to(code_0, (8, 128)), jnp.broadcast_to(code_1, (8, 128))
+        )
+        return jnp.concatenate([modes.astype(F32), code.astype(F32)], axis=0).astype(BF16)
+
     for copy in small:
         copy.wait()
-    for side in range(2):
-        for y in range(4):
-            code = jnp.where(
-                lane < 64,
-                jnp.broadcast_to(agg_v[side, 0:1, y : y + 1], (8, 128)),
-                jnp.broadcast_to(agg_v[side, 1:2, y : y + 1], (8, 128)),
-            )
-            tile = jnp.concatenate([tent_v[side, y].astype(F32), code.astype(F32)], axis=0)
-            pack_v[side, y] = tile.astype(BF16)
-
-    pl.semaphore_wait(barrier, len(peers))
-    seed_x = [
-        send(pack_v.at[0], hx_v.at[0], (outer, gy)),
-        send(pack_v.at[1], hx_v.at[1], (partner, gy)),
-    ]
-    seed_y = [
-        send(pack_v.at[:, 0], hy_v.at[1], (gx, below)),
-        send(pack_v.at[:, 3], hy_v.at[0], (gx, above)),
-    ]
 
     for y in range(4):
-        both = jnp.concatenate([pack_v[0, y], pack_v[1, y]], axis=1)
-        st_v[y] = expand(both)
+        row = pl.ds(y, 1)
+        tiles = [
+            packed(tent_v[side, y], agg_v[side, 0:1, row], agg_v[side, 1:2, row])
+            for side in range(2)
+        ]
+        st_v[y] = expand(jnp.concatenate(tiles, axis=1))
 
     for copy in big:
         copy.wait()
@@ -194,13 +245,9 @@
                 toward_i = jnp.where(keep, toward_i, 0.0)
                 toward_m = jnp.where(keep, toward_m, 0.0)
                 toward_p = jnp.where(keep, toward_p, 0.0)
-                if y == 0:
-                    toward_m = jnp.where(has_below, toward_m, 0.0)
-                if y == 3:
-                    toward_p = jnp.where(has_above, toward_p, 0.0)
                 if side == 0:
                     put(0, y, place, own, toward_i)
-                    put(1, y, place, jnp.where(has_outer, toward_o, 0.0), zero)
+                    put(1, y, place, toward_o, zero)
                     put(2, y, place, toward_m, zero)
                     put(3, y, place, toward_p, zero)
                 else:
@@ -209,54 +256,57 @@
                     put(2, y, place, zero, toward_m)
                     put(3, y, place, zero, toward_p)
 
-    def first_slot(y):
-        applied = nt(st_v[y], w_v[y, 0])
+    applied = {}
+    for y in (3, 0, 1, 2):
+        total = nt(st_v[y], w_v[y, 0])
         if y > 0:
-            applied = applied + nt(st_v[y - 1], w_v[y, 2])
+            total = total + nt(st_v[y - 1], w_v[y, 2])
         if y < 3:
-            applied = applied + nt(st_v[y + 1], w_v[y, 3])
-        relaxed = nt(applied.astype(BF16), wb_v[y])
+            total = total + nt(st_v[y + 1], w_v[y, 3])
+        applied[y] = total.astype(BF16)
+    for y in (3, 0, 1, 2):
+        relaxed = nt(applied[y], wb_v[y])
         p0_v[y] = (st_v[y].astype(F32) - RELAX * relaxed).astype(BF16)
-
-    first_slot(0)
-    first_y = [send(p0_v.at[0], hp0y_v.at[1], (gx, below))]
-    first_slot(3)
-    first_y.append(send(p0_v.at[3], hp0y_v.at[0], (gx, above)))
-    first_slot(1)
-    first_slot(2)
-    first_x = [
-        send(p0_v.at[:, :, 0:128], hp0x_v.at[:, :, 0:128], (outer, gy)),
+    first = [
+        send(p0_v.at[3], hp0y_v.at[0], (gx, above), *to_above),
+        send(p0_v.at[0], hp0y_v.at[1], (gx, below), *to_below),
+        send(p0_v.at[:, :, 0:128], hp0x_v.at[:, :, 0:128], (outer, gy), *to_outer),
         send(p0_v.at[:, :, 128:256], hp0x_v.at[:, :, 128:256], (partner, gy)),
     ]
 
-    for copy in seed_x + seed_y:
-        copy.wait_recv()
-
-    def side_slots(y):
-        halo = jnp.concatenate([hx_v[0, y], hx_v[1, y]], axis=1)
-        halos, applied = [halo], [nt(halo, w_v[y, 1]).astype(BF16)]
-        if y in (0, 3):
-            end = 0 if y == 0 else 1
-            halo = jnp.concatenate([hy_v[end, 0], hy_v[end, 1]], axis=1)
-            halos.append(halo)
-            applied.append(nt(halo, w_v[y, 2 + end]).astype(BF16))
-        applied = applied[0] if len(applied) == 1 else jnp.concatenate(applied, axis=0)
-        relaxed = nt(applied, wb_v[y])
+    await_all(seeds)
+    halos, codes = {}, {}
+    for end, y in ((1, 3), (0, 0)):
+        row = pl.ds(3 - y, 1)
+        cells = [
+            [hya_v[end, x_of[side], z : z + 1, row] for z in range(2)] for side in range(2)
+        ]
+        codes[y] = cells[0] + cells[1]
+        tiles = [packed(hyt_v[end, x_of[side]], *cells[side]) for side in range(2)]
+        halos[Y_AT[y]] = jnp.concatenate(tiles, axis=1)
+    for y in (3, 0, 1, 2):
+        row = pl.ds(y, 1)
+        tiles = [
+            packed(hxt_v[side, y], hxa_v[side, 0:1, row], hxa_v[side, 1:2, row])
+            for side in range(2)
+        ]
+        halos[X_AT[y]] = jnp.concatenate(tiles, axis=1)
+    applied = {}
+    for y in (3, 0, 1, 2):
+        applied[y] = nt(halos[X_AT[y]], w_v[y, 1]).astype(BF16)
+        if y in Y_AT:
+            more = nt(halos[Y_AT[y]], w_v[y, 2 if y == 0 else 3]).astype(BF16)
+            applied[y] = jnp.concatenate([applied[y], more], axis=0)
+    for y in (3, 0, 1, 2):
+        relaxed = nt(applied[y], wb_v[y])
         for n, at in enumerate([X_AT[y]] + ([Y_AT[y]] if y in Y_AT else [])):
             values = -RELAX * relaxed[16 * n : 16 * n + MODES]
-            tile = jnp.concatenate([values, halos[n][MODES:].astype(F32)], axis=0)
+            tile = jnp.concatenate([values, halos[at][MODES:].astype(F32)], axis=0)
             pc_v[at] = tile.astype(BF16)
-
-    side_slots(0)
-    side_slots(3)
-    side_y = [
-        send(pc_v.at[0:2], hpcy_v.at[1], (gx, below)),
-        send(pc_v.at[4:6], hpcy_v.at[0], (gx, above)),
-    ]
-    side_slots(1)
-    side_slots(2)
-    side_x = [
-        send(pc_v.at[:, :, 0:128], hpcx_v.at[:, :, 0:128], (outer, gy)),
+    side = [
+        send(pc_v.at[4:6], hpcy_v.at[0], (gx, above), *to_above),
+        send(pc_v.at[0:2], hpcy_v.at[1], (gx, below), *to_below),
+        send(pc_v.at[:, :, 0:128], hpcx_v.at[:, :, 0:128], (outer, gy), *to_outer),
         send(pc_v.at[:, :, 128:256], hpcx_v.at[:, :, 128:256], (partner, gy)),
     ]
 
@@ -274,12 +324,22 @@
     def left(y, rows):
         return jnp.concatenate([p0_v[y], lx_v[y, 0 : rows - 64]], axis=0)
 
-    terms = [jnp.zeros((64, 1), F32) for slot in range(5)]
+    lane_wide = lax.broadcasted_iota(jnp.int32, (MODES, 256), 1)
+    ly = {}
+    for y in Y_AT:
+        values = pc_v[Y_AT[y]][0:MODES].astype(F32)
+        parts = [
+            jnp.where(jnp.logical_and(lane_wide >= 64 * e, lane_wide < 64 * e + 64), values, 0.0)
+            for e in range(4)
+        ]
+        ly[y] = jnp.concatenate(parts, axis=0).astype(BF16)
+
+    terms = [jnp.zeros((rows, 1), F32) for rows in (64, 64, 64, 32, 32)]
     for y in range(4):
         res = jnp.concatenate([res_v[0, y : y + 1, :], res_v[1, y : y + 1, :]], axis=1)
         blocks = [(0, p0_v[y]), (1, lx_v[y, 0:64]), (2, lx_v[y, 64:128])]
         if y in Y_AT:
-            blocks.append((3 if y == 0 else 4, lx_v[y, 128:192]))
+            blocks.append((3 if y == 0 else 4, ly[y]))
         for slot, block in blocks:
             terms[slot] = terms[slot] + jnp.sum(block.astype(F32) * res, axis=1, keepdims=True)
 
@@ -295,8 +355,7 @@
             size = 256 if y + 1 in Y_AT else 192
             acc_v[y, 0:size] = acc_v[y, 0:size] + nt(left(y + 1, size), w_v[y, 3])
 
-    for copy in first_x + first_y:
-        copy.wait_recv()
+    await_all(first)
     for y in range(4):
         part = nt(hp0x_v[y], w_v[y, 1])
         acc_v[y, 64:128, 0:128] = acc_v[y, 64:128, 0:128] + part[:, 0:128]
@@ -305,8 +364,7 @@
             end = 0 if y == 0 else 1
             acc_v[y, 192:256] = acc_v[y, 192:256] + nt(hp0y_v[end], w_v[y, 2 + end])
 
-    for copy in side_y + side_x:
-        copy.wait_recv()
+    await_all(side)
 
     def finish(y):
         if y in Y_AT:
@@ -323,7 +381,7 @@
             right = jnp.concatenate(
                 [own, mid[128:192], corner_o, mid[0:64], corner_i, mid[64:128]], axis=0
             )
-            return nt(left(y, 256), right)
+            return nt(jnp.concatenate([left(y, 192), ly[y]], axis=0), right)
         partx = nt(expand(hpcx_v[X_AT[y]]), w_v[y, 1])
         own = (acc_v[y, 0:64] + partx).astype(BF16)
         mid = acc_v[y, 64:256].astype(BF16)
@@ -331,15 +389,23 @@
         return nt(left(y, 192), right)
 
     def pick(first, second):
-        return jnp.where(low, first, second)
+        shape = first.shape if hasattr(first, "shape") else second.shape
+        return jnp.where(wide[0 : shape[0]] < 64, first, second)
 
     def half(tile, near):
-        moved = jnp.where(low, tile, pltpu.roll(tile, 96, 1))
+        moved = pick(tile, pltpu.roll(tile, 96, 1))
         return jnp.where(is_odd, moved, tile) if near else jnp.where(is_odd, tile, moved)
 
     def with_terms(tile, term):
         upper = term.astype(BF16).astype(F32)
-        return jnp.where(wide == 96, upper, jnp.where(wide == 97, term - upper, tile))
+        at = wide[0 : tile.shape[0]]
+        return jnp.where(at == 96, upper, jnp.where(at == 97, term - upper, tile))
+
+    def with_codes(tile, y):
+        column = jnp.concatenate(
+            [jnp.broadcast_to(cell, (MODES, 128)) for cell in codes[y]], axis=0
+        )
+        return jnp.where(wide[0:32] == 112, column.astype(F32), tile)
 
     def tiles(product, slot):
         rows = product[slot * 64 : slot * 64 + 64]
@@ -349,22 +415,22 @@
         for n, value in enumerate(values):
             snd_v[at + n] = value.astype(BF16)
 
-    g0 = finish(0)
-    t0, t1, t2 = tiles(g0, 3)
-    post(8, [with_terms(half(pick(jnp.where(is_odd, t0, 0.0), t0), True), terms[3]), t1])
-    post(10, [half(pick(jnp.where(is_odd, 0.0, t0), t0), False), t2])
-    msgs = [
-        send(snd_v.at[8:10], rcv_v.at[8:10], (gx, below)),
-        send(snd_v.at[10:12], rcv_v.at[10:12], (partner, below)),
-    ]
-    g3 = finish(3)
-    t0, t1, t2 = tiles(g3, 3)
-    post(12, [with_terms(half(pick(jnp.where(is_odd, 0.0, t0), t0), True), terms[4]), t1])
-    post(14, [half(pick(jnp.where(is_odd, t0, 0.0), t0), False), t2])
-    msgs += [
-        send(snd_v.at[12:14], rcv_v.at[12:14], (gx, above)),
-        send(snd_v.at[14:16], rcv_v.at[14:16], (partner, above)),
-    ]
+    msgs = []
+    g3, g0 = finish(3), finish(0)
+    for end, g, y, peer, way in ((1, g3, 3, above, to_above), (0, g0, 0, below, to_below)):
+        t0, t1, t2 = [g[192:224, 128 * t : 128 * t + 128] for t in range(3)]
+        kept = (jnp.where(is_odd, 0.0, t0), t0) if end else (jnp.where(is_odd, t0, 0.0), t0)
+        near = half(pick(*kept), True)
+        kept = (jnp.where(is_odd, t0, 0.0), t0) if end else (jnp.where(is_odd, 0.0, t0), t0)
+        far = half(pick(*kept), False)
+        sny_v[end, 0] = with_codes(with_terms(near, terms[3 + end]), y).astype(BF16)
+        sny_v[end, 1] = t1.astype(BF16)
+        sny_v[end, 2] = with_codes(far, y).astype(BF16)
+        sny_v[end, 3] = t2.astype(BF16)
+        msgs += [
+            send(sny_v.at[end, 0:2], rcy_v.at[1 - end, 0:2], (gx, peer), *way),
+            send(sny_v.at[end, 2:4], rcy_v.at[1 - end, 2:4], (partner, peer), *way),
+        ]
     g1 = finish(1)
     g2 = finish(2)
 
@@ -391,8 +457,8 @@
     )
     post(7, [half(pick(by_side(om, op), o_sum), True)])
     msgs += [
-        send(snd_v.at[4:7], rcv_v.at[4:7], (outer, gy)),
-        send(snd_v.at[7:8], rcv_v.at[7:8], (outer2, gy)),
+        send(snd_v.at[4:7], rcv_v.at[4:7], (outer, gy), *to_outer),
+        send(snd_v.at[7:8], rcv_v.at[7:8], (outer2, gy), *to_outer2),
     ]
     um, up, mid, om, op, o_sum, im, ip, i_sum = summed(2)
     post(3, [with_terms(half(pick(by_side(ip, im), i_sum), False), terms[2])])
@@ -413,19 +479,31 @@
     own_b = swap(pick(op, o_sum))
     own_c = pick(om, 0.0)
 
-    for copy in msgs:
-        copy.wait_recv()
+    await_all(msgs)
 
     def got(at):
         return rcv_v[at].astype(F32)
 
-    y_near, y_far = got(13), got(15)
-    own_a = own_a + got(3) + got(4) + got(8) + got(12)
-    own_b = own_b + got(5) + got(9) + pick(y_near, 0.0)
-    own_c = own_c + got(6) + pick(swap(y_near), 0.0)
-    far_a = far_a + got(0) + got(7) + got(10) + got(14)
-    far_b = far_b + got(1) + got(11) + pick(y_far, 0.0)
-    far_c = far_c + got(2) + pick(swap(y_far), 0.0)
+    def spread(end, at):
+        first, second = rcy_v[end, at].astype(F32), rcy_v[end, at + 1].astype(F32)
+        code = jnp.broadcast_to(first[:, 112:113], (32, 128))
+        results = []
+        for tile in (first, second):
+            rows = []
+            for a in range(AGG):
+                here = jnp.where(code == float(a), tile, 0.0)
+                rows.append(here[0:8] + here[8:16] + here[16:24] + here[24:32])
+            results.append(jnp.concatenate(rows, axis=0))
+        return results
+
+    (up_a, up_b), (down_a, down_b) = spread(1, 0), spread(0, 0)
+    own_a = own_a + got(3) + got(4) + up_a + down_a
+    own_b = own_b + got(5) + up_b + pick(down_b, 0.0)
+    own_c = own_c + got(6) + pick(swap(down_b), 0.0)
+    (up_a, up_b), (down_a, down_b) = spread(1, 2), spread(0, 2)
+    far_a = far_a + got(0) + got(7) + up_a + down_a
+    far_b = far_b + got(1) + up_b + pick(down_b, 0.0)
+    far_c = far_c + got(2) + pick(swap(down_b), 0.0)
 
     def both(own, far):
         first, second = jnp.where(is_odd, far, own), jnp.where(is_odd, own, far)
@@ -450,8 +528,8 @@
         out[608:672] = c[64:128]
         out[800:801] = swap(a[96:97] + a[97:98])
 
-    for copy in sends:
-        copy.wait_send()
+    for copy, leaves in sends:
+        only(leaves, copy.wait_send)
 
 
 def finish_kernel(data, coarse, restricted, row, sem):
@@ -480,9 +558,10 @@
         pltpu.VMEM(residual.shape, F32),
         pltpu.VMEM((4, 4, 256, 256), BF16),
         pltpu.VMEM((4, 256, 256), BF16),
-        pltpu.VMEM((2, 4, 16, 128), BF16),
-        pltpu.VMEM((2, 4, 16, 128), BF16),
-        pltpu.VMEM((2, 2, 16, 128), BF16),
+        pltpu.VMEM(tentative.shape, BF16),
+        pltpu.VMEM(aggregate.shape, jnp.int32),
+        pltpu.VMEM((2, 2, 8, 128), BF16),
+        pltpu.VMEM((2,) + aggregate.shape, jnp.int32),
         pltpu.VMEM((4, 64, 256), BF16),
         pltpu.VMEM((4, 64, 256), BF16),
         pltpu.VMEM((2, 64, 256), BF16),
@@ -492,11 +571,13 @@
         pltpu.VMEM((4, 64, 256), BF16),
         pltpu.VMEM((4, 192, 256), BF16),
         pltpu.VMEM((4, 256, 256), F32),
-        pltpu.VMEM((16, 64, 128), BF16),
-        pltpu.VMEM((16, 64, 128), BF16),
+        pltpu.VMEM((8, 64, 128), BF16),
+        pltpu.VMEM((8, 64, 128), BF16),
+        pltpu.VMEM((2, 4, 32, 128), BF16),
+        pltpu.VMEM((2, 4, 32, 128), BF16),
         pltpu.SemaphoreType.DMA((10,)),
-        pltpu.SemaphoreType.DMA((19,)),
-        pltpu.SemaphoreType.DMA((19,)),
+        pltpu.SemaphoreType.DMA((23,)),
+        pltpu.SemaphoreType.DMA((23,)),
     ]
     sizes = (lax.axis_size("gx"), lax.axis_size("gy"))
 

time: 31.2 us -> 27.4 us (0.88)
  the two profiles are of different devices: /device:TPU:1 before, /device:TPU:30 now
where the time goes in v3:
time: 27.4 us; the launch traced here: 27.2 us
  Pallas kernels  26.6 us (97%)
  between operations  0.64 us (2%)
    pallas_call x1, Pallas kernels, body(): pl.pallas_call(call, out_shape=pltpu.VMEM((808, 128), F32), in_specs=[hbm...  25.8 us
    pallas_call x1, Pallas kernels, body(): pl.pallas_call(finish_kernel, out_shape=(jax.ShapeDtypeStruct((1, 1, 800,...  0.77 us

profile of v3, /device:TPU:30, one launch (start us, length us, event | category | flops | bytes accessed | tf_op | source)
XLA Modules:
  0.0 27.2 jit_solution(11930011047717125317)
XLA Ops:
  0.6 25.8 %galerkin.1.data = f32[808,128]{1,0:T(8,128)S(1)} custom-call(bf16[2,4,2,64,448]{4,3,2,1,0:T(8,128)(2,1)} %refs_0_.1, bf16[2,4,64,128]{3,2,1,0:T(8,128)(2,1)} %refs_1_.1, bf16[2,4,8,128]{3,2,1,0:T(8,128)(2,1)} %refs_2_.1, s32[2,2,4]{2,1,0:T(2,128)} %bitcast.2, f32[2,4,128]{2,1,0:T(4,128)} %refs_4_.1), custom_call_target="tpu_custom_call" | custom-call | tf_op jit(solution)/shard_map/galerkin/pallas_call | solution.py:587
  26.4 0.8 %store.1 = (f32[1,1,800,128]{3,2,1,0:T(8,128)}, f32[1,1,64]{2,1,0:T(1,128)}) custom-call(f32[808,128]{1,0:T(8,128)S(1)} %galerkin.1.data), custom_call_target="tpu_custom_call" | custom-call | tf_op jit(solution)/shard_map/store/pallas_call | solution.py:598

commit v4 on v3

--- a/solution.py
+++ b/solution.py
@@ -19,10 +19,32 @@
     return lax.dot_general(left, right, (((1,), (1,)), ((), ())), preferred_element_type=F32)
 
 
-def expand(tile):
-    values, code = tile[0:MODES].astype(F32), tile[MODES : 2 * MODES].astype(F32)
+def nn(left, right):
+    return lax.dot_general(left, right, (((1,), (0,)), ((), ())), preferred_element_type=F32)
+
+
+def spread_columns(values, code):
     rows = [jnp.where(code == float(a), values, 0.0) for a in range(AGG)]
     return jnp.concatenate(rows, axis=0).astype(BF16)
+
+
+def expand(tile):
+    return spread_columns(tile[0:MODES].astype(F32), tile[MODES : 2 * MODES].astype(F32))
+
+
+def by_element(values):
+    lane = lax.broadcasted_iota(jnp.int32, (MODES, 256), 1)
+    parts = [
+        jnp.where(jnp.logical_and(lane >= 64 * e, lane < 64 * e + 64), values, 0.0)
+        for e in range(4)
+    ]
+    return jnp.concatenate(parts, axis=0).astype(BF16)
+
+
+def far_slot(seed, code, product):
+    rows = -RELAX * nt(by_element(seed), product)
+    parts = [rows[8 * e : 8 * e + 8] for e in range(4)]
+    return spread_columns(jnp.concatenate(parts, axis=1), code)
 
 
 def swap(tile):
@@ -45,16 +67,18 @@
     res_v,
     w_v,
     wb_v,
-    hxt_v,
-    hxa_v,
-    hyt_v,
-    hya_v,
+    pack_v,
+    hx_v,
+    hy_v,
+    hd_v,
+    k_v,
+    hkx_v,
+    hky_v,
     p0_v,
     hp0x_v,
     hp0y_v,
     pc_v,
-    hpcx_v,
-    hpcy_v,
+    corner_v,
     st_v,
     lx_v,
     acc_v,
@@ -90,8 +114,10 @@
     peers = [
         ((gx, above), has_above),
         ((partner, above), has_above),
+        ((outer, above), jnp.logical_and(has_outer, has_above)),
         ((gx, below), has_below),
         ((partner, below), has_below),
+        ((outer, below), jnp.logical_and(has_outer, has_below)),
         ((outer, gy), has_outer),
         ((outer2, gy), has_outer),
         ((back2, gy), has_back),
@@ -151,25 +177,12 @@
     to_outer, to_outer2 = (has_outer, has_outer), (has_outer, has_back)
     to_below, to_above = (has_below, has_above), (has_above, has_below)
 
-    pl.semaphore_wait(barrier, awaited)
-    x_of = [odd, 1 - odd]
-    seeds = [
-        send(tentative.at[:, 3], hyt_v.at[0], (gx, above), *to_above),
-        send(aggregate, hya_v.at[0], (gx, above), *to_above),
-        send(tentative.at[:, 0], hyt_v.at[1], (gx, below), *to_below),
-        send(aggregate, hya_v.at[1], (gx, below), *to_below),
-        send(tentative.at[x_of[0]], hxt_v.at[0], (outer, gy), *to_outer),
-        send(aggregate.at[x_of[0]], hxa_v.at[0], (outer, gy), *to_outer),
-        send(tentative.at[x_of[1]], hxt_v.at[1], (partner, gy)),
-        send(aggregate.at[x_of[1]], hxa_v.at[1], (partner, gy)),
-    ]
-
     @pl.when(jnp.logical_not(has_outer))
     def _():
-        hxt_v[0] = jnp.zeros(hxt_v.shape[1:], BF16)
-        hxa_v[0] = jnp.zeros(hxa_v.shape[1:], jnp.int32)
+        hx_v[0] = jnp.zeros(hx_v.shape[1:], BF16)
+        hd_v[:, 0] = jnp.zeros((2, 16, 128), BF16)
+        hkx_v[:, :, 0:128] = jnp.zeros((6, 64, 128), BF16)
         hp0x_v[:, :, 0:128] = jnp.zeros((4, 64, 128), BF16)
-        hpcx_v[:, :, 0:128] = jnp.zeros((6, 16, 128), BF16)
         rcv_v[4:7] = jnp.zeros((3, 64, 128), BF16)
 
     @pl.when(jnp.logical_not(has_back))
@@ -180,10 +193,10 @@
 
         @pl.when(jnp.logical_not(condition))
         def _(end=end):
-            hyt_v[end] = jnp.zeros(hyt_v.shape[1:], BF16)
-            hya_v[end] = jnp.zeros(hya_v.shape[1:], jnp.int32)
+            hy_v[end] = jnp.zeros((2, 16, 128), BF16)
+            hd_v[end] = jnp.zeros((2, 16, 128), BF16)
+            hky_v[end] = jnp.zeros((2, 64, 256), BF16)
             hp0y_v[end] = jnp.zeros((64, 256), BF16)
-            hpcy_v[end] = jnp.zeros((2, 16, 256), BF16)
             rcy_v[end] = jnp.zeros((4, 32, 128), BF16)
 
     lane = lax.broadcasted_iota(jnp.int32, (8, 128), 1)
@@ -196,13 +209,16 @@
     for copy in small:
         copy.wait()
 
+    own = {}
     for y in range(4):
         row = pl.ds(y, 1)
-        tiles = [
-            packed(tent_v[side, y], agg_v[side, 0:1, row], agg_v[side, 1:2, row])
-            for side in range(2)
-        ]
-        st_v[y] = expand(jnp.concatenate(tiles, axis=1))
+        tiles = []
+        for side in range(2):
+            tile = packed(tent_v[side, y], agg_v[side, 0:1, row], agg_v[side, 1:2, row])
+            pack_v[side, y] = tile
+            tiles.append(tile)
+        own[y] = jnp.concatenate(tiles, axis=1).astype(F32)
+        st_v[y] = expand(own[y])
 
     for copy in big:
         copy.wait()
@@ -232,12 +248,12 @@
                 d = jnp.concatenate([d, d], axis=1)
                 ra, rb, rc = swap(a), swap(b), swap(c)
                 if z == 0:
-                    own = jnp.where(low, a, d)
+                    centre = jnp.where(low, a, d)
                     toward_o, toward_i = jnp.where(is_odd, b, ra), jnp.where(is_odd, ra, b)
                     toward_m, toward_p = rb, c
                     keep = low
                 else:
-                    own = jnp.where(low, rc, ra)
+                    centre = jnp.where(low, rc, ra)
                     toward_o, toward_i = jnp.where(is_odd, rb, a), jnp.where(is_odd, a, rb)
                     toward_m, toward_p = b, rc
                     keep = jnp.logical_not(low)
@@ -246,15 +262,41 @@
                 toward_m = jnp.where(keep, toward_m, 0.0)
                 toward_p = jnp.where(keep, toward_p, 0.0)
                 if side == 0:
-                    put(0, y, place, own, toward_i)
+                    put(0, y, place, centre, toward_i)
                     put(1, y, place, toward_o, zero)
                     put(2, y, place, toward_m, zero)
                     put(3, y, place, toward_p, zero)
                 else:
-                    put(0, y, place, toward_o, own)
+                    put(0, y, place, toward_o, centre)
                     put(1, y, place, zero, toward_i)
                     put(2, y, place, zero, toward_m)
                     put(3, y, place, zero, toward_p)
+
+    for y in range(4):
+        blocks = jnp.concatenate([inv_v[0, y], inv_v[1, y]], axis=1)
+        k_v[X_AT[y]] = nn(blocks, w_v[y, 1]).astype(BF16)
+        if y in Y_AT:
+            k_v[Y_AT[y]] = nn(blocks, w_v[y, 2 if y == 0 else 3]).astype(BF16)
+
+    pl.semaphore_wait(barrier, awaited)
+    corner_above = (jnp.logical_and(has_outer, has_above), jnp.logical_and(has_outer, has_below))
+    corner_below = (corner_above[1], corner_above[0])
+    seeds = [
+        send(pack_v.at[:, 3], hy_v.at[0], (gx, above), *to_above),
+        send(pack_v.at[0, 3], hd_v.at[0, 0], (outer, above), *corner_above),
+        send(pack_v.at[1, 3], hd_v.at[0, 1], (partner, above), *to_above),
+        send(pack_v.at[:, 0], hy_v.at[1], (gx, below), *to_below),
+        send(pack_v.at[0, 0], hd_v.at[1, 0], (outer, below), *corner_below),
+        send(pack_v.at[1, 0], hd_v.at[1, 1], (partner, below), *to_below),
+        send(pack_v.at[0], hx_v.at[0], (outer, gy), *to_outer),
+        send(pack_v.at[1], hx_v.at[1], (partner, gy)),
+    ]
+    products = [
+        send(k_v.at[4:6], hky_v.at[0], (gx, above), *to_above),
+        send(k_v.at[0:2], hky_v.at[1], (gx, below), *to_below),
+        send(k_v.at[:, :, 0:128], hkx_v.at[:, :, 0:128], (outer, gy), *to_outer),
+        send(k_v.at[:, :, 128:256], hkx_v.at[:, :, 128:256], (partner, gy)),
+    ]
 
     applied = {}
     for y in (3, 0, 1, 2):
@@ -275,22 +317,12 @@
     ]
 
     await_all(seeds)
-    halos, codes = {}, {}
+    halos, corners = {}, {}
     for end, y in ((1, 3), (0, 0)):
-        row = pl.ds(3 - y, 1)
-        cells = [
-            [hya_v[end, x_of[side], z : z + 1, row] for z in range(2)] for side in range(2)
-        ]
-        codes[y] = cells[0] + cells[1]
-        tiles = [packed(hyt_v[end, x_of[side]], *cells[side]) for side in range(2)]
-        halos[Y_AT[y]] = jnp.concatenate(tiles, axis=1)
+        halos[Y_AT[y]] = jnp.concatenate([hy_v[end, 0], hy_v[end, 1]], axis=1)
+        corners[y] = jnp.concatenate([hd_v[end, 0], hd_v[end, 1]], axis=1).astype(F32)
     for y in (3, 0, 1, 2):
-        row = pl.ds(y, 1)
-        tiles = [
-            packed(hxt_v[side, y], hxa_v[side, 0:1, row], hxa_v[side, 1:2, row])
-            for side in range(2)
-        ]
-        halos[X_AT[y]] = jnp.concatenate(tiles, axis=1)
+        halos[X_AT[y]] = jnp.concatenate([hx_v[0, y], hx_v[1, y]], axis=1)
     applied = {}
     for y in (3, 0, 1, 2):
         applied[y] = nt(halos[X_AT[y]], w_v[y, 1]).astype(BF16)
@@ -303,12 +335,6 @@
             values = -RELAX * relaxed[16 * n : 16 * n + MODES]
             tile = jnp.concatenate([values, halos[at][MODES:].astype(F32)], axis=0)
             pc_v[at] = tile.astype(BF16)
-    side = [
-        send(pc_v.at[4:6], hpcy_v.at[0], (gx, above), *to_above),
-        send(pc_v.at[0:2], hpcy_v.at[1], (gx, below), *to_below),
-        send(pc_v.at[:, :, 0:128], hpcx_v.at[:, :, 0:128], (outer, gy), *to_outer),
-        send(pc_v.at[:, :, 128:256], hpcx_v.at[:, :, 128:256], (partner, gy)),
-    ]
 
     out[...] = jnp.zeros(out.shape, F32)
     blank = jnp.zeros((64, 128), BF16)
@@ -324,15 +350,7 @@
     def left(y, rows):
         return jnp.concatenate([p0_v[y], lx_v[y, 0 : rows - 64]], axis=0)
 
-    lane_wide = lax.broadcasted_iota(jnp.int32, (MODES, 256), 1)
-    ly = {}
-    for y in Y_AT:
-        values = pc_v[Y_AT[y]][0:MODES].astype(F32)
-        parts = [
-            jnp.where(jnp.logical_and(lane_wide >= 64 * e, lane_wide < 64 * e + 64), values, 0.0)
-            for e in range(4)
-        ]
-        ly[y] = jnp.concatenate(parts, axis=0).astype(BF16)
+    ly = {y: by_element(pc_v[Y_AT[y]][0:MODES].astype(F32)) for y in Y_AT}
 
     terms = [jnp.zeros((rows, 1), F32) for rows in (64, 64, 64, 32, 32)]
     for y in range(4):
@@ -355,38 +373,44 @@
             size = 256 if y + 1 in Y_AT else 192
             acc_v[y, 0:size] = acc_v[y, 0:size] + nt(left(y + 1, size), w_v[y, 3])
 
-    await_all(first)
-    for y in range(4):
-        part = nt(hp0x_v[y], w_v[y, 1])
-        acc_v[y, 64:128, 0:128] = acc_v[y, 64:128, 0:128] + part[:, 0:128]
-        acc_v[y, 128:192, 128:256] = acc_v[y, 128:192, 128:256] + part[:, 128:256]
+    await_all(products)
+    for y in (3, 0, 1, 2):
+        seed, code = own[y][0:MODES], own[y][MODES:]
+        fromx = far_slot(seed, code, hkx_v[X_AT[y]])
         if y in Y_AT:
             end = 0 if y == 0 else 1
-            acc_v[y, 192:256] = acc_v[y, 192:256] + nt(hp0y_v[end], w_v[y, 2 + end])
-
-    await_all(side)
+            far_seed, far_code = corners[y][0:MODES], corners[y][MODES:]
+            more = far_slot(far_seed, far_code, hkx_v[Y_AT[y]])
+            partx = nt(jnp.concatenate([fromx, more], axis=0), w_v[y, 1])
+            fromy = [
+                far_slot(far_seed, far_code, hky_v[end, 0]),
+                far_slot(seed, code, hky_v[end, 1]),
+            ]
+            party = nt(jnp.concatenate(fromy, axis=0), w_v[y, 2 + end])
+            acc_v[y, 0:64] = acc_v[y, 0:64] + partx[0:64] + party[64:128]
+            corner_v[end] = (partx[64:128] + party[0:64]).astype(BF16)
+        else:
+            acc_v[y, 0:64] = acc_v[y, 0:64] + nt(fromx, w_v[y, 1])
+
+    await_all(first)
 
     def finish(y):
-        if y in Y_AT:
-            end = 0 if y == 0 else 1
-            fromx = jnp.concatenate([expand(hpcx_v[X_AT[y]]), expand(hpcx_v[Y_AT[y]])], axis=0)
-            partx = nt(fromx, w_v[y, 1])
-            fromy = jnp.concatenate([expand(hpcy_v[end, 0]), expand(hpcy_v[end, 1])], axis=0)
-            party = nt(fromy, w_v[y, 2 + end])
-            own = (acc_v[y, 0:64] + partx[0:64] + party[64:128]).astype(BF16)
-            corner = (partx[64:128] + party[0:64]).astype(BF16)
-            mid = acc_v[y, 64:256].astype(BF16)
-            corner_o = jnp.concatenate([corner[:, 0:128], blank], axis=1)
-            corner_i = jnp.concatenate([blank, corner[:, 128:256]], axis=1)
-            right = jnp.concatenate(
-                [own, mid[128:192], corner_o, mid[0:64], corner_i, mid[64:128]], axis=0
-            )
-            return nt(jnp.concatenate([left(y, 192), ly[y]], axis=0), right)
-        partx = nt(expand(hpcx_v[X_AT[y]]), w_v[y, 1])
-        own = (acc_v[y, 0:64] + partx).astype(BF16)
-        mid = acc_v[y, 64:256].astype(BF16)
-        right = jnp.concatenate([own, mid[128:192], mid[64:128], mid[0:64]], axis=0)
-        return nt(left(y, 192), right)
+        part = nt(hp0x_v[y], w_v[y, 1])
+        row_0 = acc_v[y, 0:64].astype(BF16)
+        row_o, row_i, row_y = acc_v[y, 64:128], acc_v[y, 128:192], acc_v[y, 192:256]
+        row_o = jnp.concatenate([row_o[:, 0:128] + part[:, 0:128], row_o[:, 128:256]], axis=1)
+        row_i = jnp.concatenate([row_i[:, 0:128], row_i[:, 128:256] + part[:, 128:256]], axis=1)
+        row_o, row_i = row_o.astype(BF16), row_i.astype(BF16)
+        if y not in Y_AT:
+            right = jnp.concatenate([row_0, row_y.astype(BF16), row_i, row_o], axis=0)
+            return nt(left(y, 192), right)
+        end = 0 if y == 0 else 1
+        row_y = (row_y + nt(hp0y_v[end], w_v[y, 2 + end])).astype(BF16)
+        corner = corner_v[end]
+        corner_o = jnp.concatenate([corner[:, 0:128], blank], axis=1)
+        corner_i = jnp.concatenate([blank, corner[:, 128:256]], axis=1)
+        right = jnp.concatenate([row_0, row_y, corner_o, row_o, corner_i, row_i], axis=0)
+        return nt(jnp.concatenate([left(y, 192), ly[y]], axis=0), right)
 
     def pick(first, second):
         shape = first.shape if hasattr(first, "shape") else second.shape
@@ -402,10 +426,12 @@
         return jnp.where(at == 96, upper, jnp.where(at == 97, term - upper, tile))
 
     def with_codes(tile, y):
+        code = halos[Y_AT[y]][MODES:].astype(F32)
+        cells = [code[:, 64 * e : 64 * e + 1] for e in range(4)]
         column = jnp.concatenate(
-            [jnp.broadcast_to(cell, (MODES, 128)) for cell in codes[y]], axis=0
+            [jnp.broadcast_to(cell, (MODES, 128)) for cell in cells], axis=0
         )
-        return jnp.where(wide[0:32] == 112, column.astype(F32), tile)
+        return jnp.where(wide[0:32] == 112, column, tile)
 
     def tiles(product, slot):
         rows = product[slot * 64 : slot * 64 + 64]
@@ -558,16 +584,18 @@
         pltpu.VMEM(residual.shape, F32),
         pltpu.VMEM((4, 4, 256, 256), BF16),
         pltpu.VMEM((4, 256, 256), BF16),
-        pltpu.VMEM(tentative.shape, BF16),
-        pltpu.VMEM(aggregate.shape, jnp.int32),
-        pltpu.VMEM((2, 2, 8, 128), BF16),
-        pltpu.VMEM((2,) + aggregate.shape, jnp.int32),
+        pltpu.VMEM((2, 4, 16, 128), BF16),
+        pltpu.VMEM((2, 4, 16, 128), BF16),
+        pltpu.VMEM((2, 2, 16, 128), BF16),
+        pltpu.VMEM((2, 2, 16, 128), BF16),
+        pltpu.VMEM((6, 64, 256), BF16),
+        pltpu.VMEM((6, 64, 256), BF16),
+        pltpu.VMEM((2, 2, 64, 256), BF16),
         pltpu.VMEM((4, 64, 256), BF16),
         pltpu.VMEM((4, 64, 256), BF16),
         pltpu.VMEM((2, 64, 256), BF16),
         pltpu.VMEM((6, 16, 256), BF16),
-        pltpu.VMEM((6, 16, 256), BF16),
-        pltpu.VMEM((2, 2, 16, 256), BF16),
+        pltpu.VMEM((2, 64, 256), BF16),
         pltpu.VMEM((4, 64, 256), BF16),
         pltpu.VMEM((4, 192, 256), BF16),
         pltpu.VMEM((4, 256, 256), F32),

time: 27.4 us -> 24.7 us (0.901)
  Pallas kernels: 26.6 us -> 23.9 us
    pallas_call x1, Pallas kernels: 25.8 us -> 23.1 us  [body(): pl.pallas_call(call, out_shape=pltpu.VMEM((808, 128), F32), in_specs=[hbm...]
where the time goes in v4:
time: 24.7 us; the launch traced here: 24.5 us
  Pallas kernels  23.9 us (97%)
  between operations  0.64 us (3%)
    pallas_call x1, Pallas kernels, body(): pl.pallas_call(call, out_shape=pltpu.VMEM((808, 128), F32), in_specs=[hbm...  23.1 us
    pallas_call x1, Pallas kernels, body(): pl.pallas_call(finish_kernel, out_shape=(jax.ShapeDtypeStruct((1, 1, 800,...  0.77 us

profile of v4, /device:TPU:30, one launch (start us, length us, event | category | flops | bytes accessed | tf_op | source)
XLA Modules:
  0.0 24.5 jit_solution(12347401916989751796)
XLA Ops:
  0.6 23.1 %galerkin.1.data = f32[808,128]{1,0:T(8,128)S(1)} custom-call(bf16[2,4,2,64,448]{4,3,2,1,0:T(8,128)(2,1)} %refs_0_.1, bf16[2,4,64,128]{3,2,1,0:T(8,128)(2,1)} %refs_1_.1, bf16[2,4,8,128]{3,2,1,0:T(8,128)(2,1)} %refs_2_.1, s32[2,2,4]{2,1,0:T(2,128)} %bitcast.2, f32[2,4,128]{2,1,0:T(4,128)} %refs_4_.1), custom_call_target="tpu_custom_call" | custom-call | tf_op jit(solution)/shard_map/galerkin/pallas_call | solution.py:615
  23.8 0.8 %store.1 = (f32[1,1,800,128]{3,2,1,0:T(8,128)}, f32[1,1,64]{2,1,0:T(1,128)}) custom-call(f32[808,128]{1,0:T(8,128)S(1)} %galerkin.1.data), custom_call_target="tpu_custom_call" | custom-call | tf_op jit(solution)/shard_map/store/pallas_call | solution.py:626

commit v5 on v4

--- a/solution.py
+++ b/solution.py
@@ -41,10 +41,10 @@
     return jnp.concatenate(parts, axis=0).astype(BF16)
 
 
-def far_slot(seed, code, product):
-    rows = -RELAX * nt(by_element(seed), product)
-    parts = [rows[8 * e : 8 * e + 8] for e in range(4)]
-    return spread_columns(jnp.concatenate(parts, axis=1), code)
+def slot_values(seeds, product):
+    rows = -RELAX * nt(seeds, product)
+    values = jnp.concatenate([rows[8 * e : 8 * e + 8] for e in range(4)], axis=1)
+    return values.astype(BF16).astype(F32)
 
 
 def swap(tile):
@@ -77,8 +77,6 @@
     p0_v,
     hp0x_v,
     hp0y_v,
-    pc_v,
-    corner_v,
     st_v,
     lx_v,
     acc_v,
@@ -278,6 +276,17 @@
         if y in Y_AT:
             k_v[Y_AT[y]] = nn(blocks, w_v[y, 2 if y == 0 else 3]).astype(BF16)
 
+    applied = {}
+    for y in (3, 0, 1, 2):
+        total = nt(st_v[y], w_v[y, 0])
+        if y > 0:
+            total = total + nt(st_v[y - 1], w_v[y, 2])
+        if y < 3:
+            total = total + nt(st_v[y + 1], w_v[y, 3])
+        applied[y] = total.astype(BF16)
+    for y in (3, 0, 1, 2):
+        relaxed = nt(applied[y], wb_v[y])
+        p0_v[y] = (st_v[y].astype(F32) - RELAX * relaxed).astype(BF16)
     pl.semaphore_wait(barrier, awaited)
     corner_above = (jnp.logical_and(has_outer, has_above), jnp.logical_and(has_outer, has_below))
     corner_below = (corner_above[1], corner_above[0])
@@ -298,17 +307,6 @@
         send(k_v.at[:, :, 128:256], hkx_v.at[:, :, 128:256], (partner, gy)),
     ]
 
-    applied = {}
-    for y in (3, 0, 1, 2):
-        total = nt(st_v[y], w_v[y, 0])
-        if y > 0:
-            total = total + nt(st_v[y - 1], w_v[y, 2])
-        if y < 3:
-            total = total + nt(st_v[y + 1], w_v[y, 3])
-        applied[y] = total.astype(BF16)
-    for y in (3, 0, 1, 2):
-        relaxed = nt(applied[y], wb_v[y])
-        p0_v[y] = (st_v[y].astype(F32) - RELAX * relaxed).astype(BF16)
     first = [
         send(p0_v.at[3], hp0y_v.at[0], (gx, above), *to_above),
         send(p0_v.at[0], hp0y_v.at[1], (gx, below), *to_below),
@@ -316,41 +314,32 @@
         send(p0_v.at[:, :, 128:256], hp0x_v.at[:, :, 128:256], (partner, gy)),
     ]
 
+    out[...] = jnp.zeros(out.shape, F32)
+    seeds_by = {y: by_element(own[y][0:MODES]) for y in range(4)}
+    blank = jnp.zeros((64, 128), BF16)
+
     await_all(seeds)
     halos, corners = {}, {}
     for end, y in ((1, 3), (0, 0)):
-        halos[Y_AT[y]] = jnp.concatenate([hy_v[end, 0], hy_v[end, 1]], axis=1)
+        halos[Y_AT[y]] = jnp.concatenate([hy_v[end, 0], hy_v[end, 1]], axis=1).astype(F32)
         corners[y] = jnp.concatenate([hd_v[end, 0], hd_v[end, 1]], axis=1).astype(F32)
-    for y in (3, 0, 1, 2):
-        halos[X_AT[y]] = jnp.concatenate([hx_v[0, y], hx_v[1, y]], axis=1)
-    applied = {}
-    for y in (3, 0, 1, 2):
-        applied[y] = nt(halos[X_AT[y]], w_v[y, 1]).astype(BF16)
-        if y in Y_AT:
-            more = nt(halos[Y_AT[y]], w_v[y, 2 if y == 0 else 3]).astype(BF16)
-            applied[y] = jnp.concatenate([applied[y], more], axis=0)
-    for y in (3, 0, 1, 2):
-        relaxed = nt(applied[y], wb_v[y])
-        for n, at in enumerate([X_AT[y]] + ([Y_AT[y]] if y in Y_AT else [])):
-            values = -RELAX * relaxed[16 * n : 16 * n + MODES]
-            tile = jnp.concatenate([values, halos[at][MODES:].astype(F32)], axis=0)
-            pc_v[at] = tile.astype(BF16)
-
-    out[...] = jnp.zeros(out.shape, F32)
-    blank = jnp.zeros((64, 128), BF16)
     for y in range(4):
-        full = expand(pc_v[X_AT[y]])
-        lx_v[y, 0:64, 0:128] = full[:, 0:128]
+        halos[X_AT[y]] = jnp.concatenate([hx_v[0, y], hx_v[1, y]], axis=1).astype(F32)
+    values = {at: slot_values(by_element(halos[at][0:MODES]), k_v[at]) for at in halos}
+    full = {at: spread_columns(values[at], halos[at][MODES:]) for at in halos}
+    corners_by = {y: by_element(corners[y][0:MODES]) for y in Y_AT}
+    ly = {y: by_element(values[Y_AT[y]]) for y in Y_AT}
+    for y in range(4):
+        slot = full[X_AT[y]]
+        lx_v[y, 0:64, 0:128] = slot[:, 0:128]
         lx_v[y, 0:64, 128:256] = blank
         lx_v[y, 64:128, 0:128] = blank
-        lx_v[y, 64:128, 128:256] = full[:, 128:256]
+        lx_v[y, 64:128, 128:256] = slot[:, 128:256]
         if y in Y_AT:
-            lx_v[y, 128:192] = expand(pc_v[Y_AT[y]])
+            lx_v[y, 128:192] = full[Y_AT[y]]
 
     def left(y, rows):
         return jnp.concatenate([p0_v[y], lx_v[y, 0 : rows - 64]], axis=0)
-
-    ly = {y: by_element(pc_v[Y_AT[y]][0:MODES].astype(F32)) for y in Y_AT}
 
     terms = [jnp.zeros((rows, 1), F32) for rows in (64, 64, 64, 32, 32)]
     for y in range(4):
@@ -374,43 +363,45 @@
             acc_v[y, 0:size] = acc_v[y, 0:size] + nt(left(y + 1, size), w_v[y, 3])
 
     await_all(products)
+    near_x, near_y, far_x, far_y = {}, {}, {}, {}
     for y in (3, 0, 1, 2):
-        seed, code = own[y][0:MODES], own[y][MODES:]
-        fromx = far_slot(seed, code, hkx_v[X_AT[y]])
-        if y in Y_AT:
-            end = 0 if y == 0 else 1
-            far_seed, far_code = corners[y][0:MODES], corners[y][MODES:]
-            more = far_slot(far_seed, far_code, hkx_v[Y_AT[y]])
-            partx = nt(jnp.concatenate([fromx, more], axis=0), w_v[y, 1])
-            fromy = [
-                far_slot(far_seed, far_code, hky_v[end, 0]),
-                far_slot(seed, code, hky_v[end, 1]),
-            ]
-            party = nt(jnp.concatenate(fromy, axis=0), w_v[y, 2 + end])
-            acc_v[y, 0:64] = acc_v[y, 0:64] + partx[0:64] + party[64:128]
-            corner_v[end] = (partx[64:128] + party[0:64]).astype(BF16)
-        else:
-            acc_v[y, 0:64] = acc_v[y, 0:64] + nt(fromx, w_v[y, 1])
+        near_x[y] = slot_values(seeds_by[y], hkx_v[X_AT[y]])
+    for end, y in ((1, 3), (0, 0)):
+        near_y[y] = slot_values(seeds_by[y], hky_v[end, 1])
+        far_x[y] = slot_values(corners_by[y], hkx_v[Y_AT[y]])
+        far_y[y] = slot_values(corners_by[y], hky_v[end, 0])
+    near_x = {y: spread_columns(near_x[y], own[y][MODES:]) for y in range(4)}
+    near_y = {y: spread_columns(near_y[y], own[y][MODES:]) for y in Y_AT}
+    far_x = {y: spread_columns(far_x[y], corners[y][MODES:]) for y in Y_AT}
+    far_y = {y: spread_columns(far_y[y], corners[y][MODES:]) for y in Y_AT}
 
     await_all(first)
 
-    def finish(y):
-        part = nt(hp0x_v[y], w_v[y, 1])
-        row_0 = acc_v[y, 0:64].astype(BF16)
+    def coupled(y):
+        rows = [hp0x_v[y], near_x[y]] + ([far_x[y]] if y in Y_AT else [])
+        part = nt(jnp.concatenate(rows, axis=0), w_v[y, 1])
+        row_0 = acc_v[y, 0:64] + part[64:128]
         row_o, row_i, row_y = acc_v[y, 64:128], acc_v[y, 128:192], acc_v[y, 192:256]
-        row_o = jnp.concatenate([row_o[:, 0:128] + part[:, 0:128], row_o[:, 128:256]], axis=1)
-        row_i = jnp.concatenate([row_i[:, 0:128], row_i[:, 128:256] + part[:, 128:256]], axis=1)
+        row_o = jnp.concatenate([row_o[:, 0:128] + part[0:64, 0:128], row_o[:, 128:256]], axis=1)
+        row_i = jnp.concatenate([row_i[:, 0:128], row_i[:, 128:256] + part[0:64, 128:256]], axis=1)
         row_o, row_i = row_o.astype(BF16), row_i.astype(BF16)
         if y not in Y_AT:
-            right = jnp.concatenate([row_0, row_y.astype(BF16), row_i, row_o], axis=0)
-            return nt(left(y, 192), right)
+            rows = [row_0.astype(BF16), row_y.astype(BF16), row_i, row_o]
+            return jnp.concatenate(rows, axis=0)
         end = 0 if y == 0 else 1
-        row_y = (row_y + nt(hp0y_v[end], w_v[y, 2 + end])).astype(BF16)
-        corner = corner_v[end]
+        rows = [hp0y_v[end], far_y[y], near_y[y]]
+        more = nt(jnp.concatenate(rows, axis=0), w_v[y, 2 + end])
+        row_0, row_y = (row_0 + more[128:192]).astype(BF16), (row_y + more[0:64]).astype(BF16)
+        corner = (part[128:192] + more[64:128]).astype(BF16)
         corner_o = jnp.concatenate([corner[:, 0:128], blank], axis=1)
         corner_i = jnp.concatenate([blank, corner[:, 128:256]], axis=1)
-        right = jnp.concatenate([row_0, row_y, corner_o, row_o, corner_i, row_i], axis=0)
-        return nt(jnp.concatenate([left(y, 192), ly[y]], axis=0), right)
+        return jnp.concatenate([row_0, row_y, corner_o, row_o, corner_i, row_i], axis=0)
+
+    right = {y: coupled(y) for y in (3, 0, 1, 2)}
+    g3 = nt(jnp.concatenate([left(3, 192), ly[3]], axis=0), right[3])
+    g0 = nt(jnp.concatenate([left(0, 192), ly[0]], axis=0), right[0])
+    g1 = nt(left(1, 192), right[1])
+    g2 = nt(left(2, 192), right[2])
 
     def pick(first, second):
         shape = first.shape if hasattr(first, "shape") else second.shape
@@ -426,7 +417,7 @@
         return jnp.where(at == 96, upper, jnp.where(at == 97, term - upper, tile))
 
     def with_codes(tile, y):
-        code = halos[Y_AT[y]][MODES:].astype(F32)
+        code = halos[Y_AT[y]][MODES:]
         cells = [code[:, 64 * e : 64 * e + 1] for e in range(4)]
         column = jnp.concatenate(
             [jnp.broadcast_to(cell, (MODES, 128)) for cell in cells], axis=0
@@ -442,7 +433,6 @@
             snd_v[at + n] = value.astype(BF16)
 
     msgs = []
-    g3, g0 = finish(3), finish(0)
     for end, g, y, peer, way in ((1, g3, 3, above, to_above), (0, g0, 0, below, to_below)):
         t0, t1, t2 = [g[192:224, 128 * t : 128 * t + 128] for t in range(3)]
         kept = (jnp.where(is_odd, 0.0, t0), t0) if end else (jnp.where(is_odd, t0, 0.0), t0)
@@ -457,8 +447,6 @@
             send(sny_v.at[end, 0:2], rcy_v.at[1 - end, 0:2], (gx, peer), *way),
             send(sny_v.at[end, 2:4], rcy_v.at[1 - end, 2:4], (partner, peer), *way),
         ]
-    g1 = finish(1)
-    g2 = finish(2)
 
     def summed(slot):
         a0, a1, a2 = tiles(g0, slot)
@@ -505,8 +493,6 @@
     own_b = swap(pick(op, o_sum))
     own_c = pick(om, 0.0)
 
-    await_all(msgs)
-
     def got(at):
         return rcv_v[at].astype(F32)
 
@@ -522,14 +508,22 @@
             results.append(jnp.concatenate(rows, axis=0))
         return results
 
-    (up_a, up_b), (down_a, down_b) = spread(1, 0), spread(0, 0)
-    own_a = own_a + got(3) + got(4) + up_a + down_a
-    own_b = own_b + got(5) + up_b + pick(down_b, 0.0)
-    own_c = own_c + got(6) + pick(swap(down_b), 0.0)
-    (up_a, up_b), (down_a, down_b) = spread(1, 2), spread(0, 2)
-    far_a = far_a + got(0) + got(7) + up_a + down_a
-    far_b = far_b + got(1) + up_b + pick(down_b, 0.0)
-    far_c = far_c + got(2) + pick(swap(down_b), 0.0)
+    await_all(msgs[6:7])
+    own_a, far_a = own_a + got(3), far_a + got(0)
+    far_b, far_c = far_b + got(1), far_c + got(2)
+    await_all(msgs[2:4])
+    (near_a, near_b), (past_a, past_b) = spread(1, 0), spread(1, 2)
+    own_a, own_b = own_a + near_a, own_b + near_b
+    far_a, far_b = far_a + past_a, far_b + past_b
+    await_all(msgs[4:6])
+    own_a, own_b, own_c = own_a + got(4), own_b + got(5), own_c + got(6)
+    far_a = far_a + got(7)
+    await_all(msgs[0:2])
+    (near_a, near_b), (past_a, past_b) = spread(0, 0), spread(0, 2)
+    own_a, own_b = own_a + near_a, own_b + pick(near_b, 0.0)
+    own_c = own_c + pick(swap(near_b), 0.0)
+    far_a, far_b = far_a + past_a, far_b + pick(past_b, 0.0)
+    far_c = far_c + pick(swap(past_b), 0.0)
 
     def both(own, far):
         first, second = jnp.where(is_odd, far, own), jnp.where(is_odd, own, far)
@@ -593,8 +587,6 @@
         pltpu.VMEM((2, 2, 64, 256), BF16),
         pltpu.VMEM((4, 64, 256), BF16),
         pltpu.VMEM((4, 64, 256), BF16),
-        pltpu.VMEM((2, 64, 256), BF16),
-        pltpu.VMEM((6, 16, 256), BF16),
         pltpu.VMEM((2, 64, 256), BF16),
         pltpu.VMEM((4, 64, 256), BF16),
         pltpu.VMEM((4, 192, 256), BF16),

time: 24.7 us -> 23.9 us (0.968)
  Pallas kernels: 23.9 us -> 23.1 us
    pallas_call x1, Pallas kernels: 23.1 us -> 22.3 us  [body(): pl.pallas_call(call, out_shape=pltpu.VMEM((808, 128), F32), in_specs=[hbm...]
where the time goes in v5:
time: 23.9 us; the launch traced here: 23.7 us
  Pallas kernels  23.1 us (97%)
  between operations  0.64 us (3%)
    pallas_call x1, Pallas kernels, body(): pl.pallas_call(call, out_shape=pltpu.VMEM((808, 128), F32), in_specs=[hbm...  22.3 us
    pallas_call x1, Pallas kernels, body(): pl.pallas_call(finish_kernel, out_shape=(jax.ShapeDtypeStruct((1, 1, 800,...  0.77 us

profile of v5, /device:TPU:30, one launch (start us, length us, event | category | flops | bytes accessed | tf_op | source)
XLA Modules:
  0.0 23.7 jit_solution(12141028582459243205)
XLA Ops:
  0.6 22.3 %galerkin.1.data = f32[808,128]{1,0:T(8,128)S(1)} custom-call(bf16[2,4,2,64,448]{4,3,2,1,0:T(8,128)(2,1)} %refs_0_.1, bf16[2,4,64,128]{3,2,1,0:T(8,128)(2,1)} %refs_1_.1, bf16[2,4,8,128]{3,2,1,0:T(8,128)(2,1)} %refs_2_.1, s32[2,2,4]{2,1,0:T(2,128)} %bitcast.2, f32[2,4,128]{2,1,0:T(4,128)} %refs_4_.1), custom_call_target="tpu_custom_call" | custom-call | tf_op jit(solution)/shard_map/galerkin/pallas_call | solution.py:607
  22.9 0.8 %store.1 = (f32[1,1,800,128]{3,2,1,0:T(8,128)}, f32[1,1,64]{2,1,0:T(1,128)}) custom-call(f32[808,128]{1,0:T(8,128)S(1)} %galerkin.1.data), custom_call_target="tpu_custom_call" | custom-call | tf_op jit(solution)/shard_map/store/pallas_call | solution.py:618

commit v6 on v5

--- a/solution.py
+++ b/solution.py
@@ -45,6 +45,16 @@
     rows = -RELAX * nt(seeds, product)
     values = jnp.concatenate([rows[8 * e : 8 * e + 8] for e in range(4)], axis=1)
     return values.astype(BF16).astype(F32)
+
+
+def halves(ref, at, dim=0):
+    parts = [ref[at, n] if dim else ref[n, at] for n in range(2)]
+    return jnp.concatenate(parts, axis=1)
+
+
+def put_halves(ref, at, value):
+    ref[0, at] = value[:, 0:128].astype(BF16)
+    ref[1, at] = value[:, 128:256].astype(BF16)
 
 
 def swap(tile):
@@ -179,8 +189,8 @@
     def _():
         hx_v[0] = jnp.zeros(hx_v.shape[1:], BF16)
         hd_v[:, 0] = jnp.zeros((2, 16, 128), BF16)
-        hkx_v[:, :, 0:128] = jnp.zeros((6, 64, 128), BF16)
-        hp0x_v[:, :, 0:128] = jnp.zeros((4, 64, 128), BF16)
+        hkx_v[0] = jnp.zeros((6, 64, 128), BF16)
+        hp0x_v[0] = jnp.zeros((4, 64, 128), BF16)
         rcv_v[4:7] = jnp.zeros((3, 64, 128), BF16)
 
     @pl.when(jnp.logical_not(has_back))
@@ -193,8 +203,8 @@
         def _(end=end):
             hy_v[end] = jnp.zeros((2, 16, 128), BF16)
             hd_v[end] = jnp.zeros((2, 16, 128), BF16)
-            hky_v[end] = jnp.zeros((2, 64, 256), BF16)
-            hp0y_v[end] = jnp.zeros((64, 256), BF16)
+            hky_v[end] = jnp.zeros((2, 2, 64, 128), BF16)
+            hp0y_v[end] = jnp.zeros((2, 64, 128), BF16)
             rcy_v[end] = jnp.zeros((4, 32, 128), BF16)
 
     lane = lax.broadcasted_iota(jnp.int32, (8, 128), 1)
@@ -272,9 +282,31 @@
 
     for y in range(4):
         blocks = jnp.concatenate([inv_v[0, y], inv_v[1, y]], axis=1)
-        k_v[X_AT[y]] = nn(blocks, w_v[y, 1]).astype(BF16)
+        put_halves(k_v, X_AT[y], nn(blocks, w_v[y, 1]))
         if y in Y_AT:
-            k_v[Y_AT[y]] = nn(blocks, w_v[y, 2 if y == 0 else 3]).astype(BF16)
+            put_halves(k_v, Y_AT[y], nn(blocks, w_v[y, 2 if y == 0 else 3]))
+
+    pl.semaphore_wait(barrier, awaited)
+    corner_above = (jnp.logical_and(has_outer, has_above), jnp.logical_and(has_outer, has_below))
+    corner_below = (corner_above[1], corner_above[0])
+    seeds = [
+        send(pack_v.at[:, 3], hy_v.at[0], (gx, above), *to_above),
+        send(pack_v.at[:, 0], hy_v.at[1], (gx, below), *to_below),
+        send(pack_v.at[0], hx_v.at[0], (outer, gy), *to_outer),
+        send(pack_v.at[1], hx_v.at[1], (partner, gy)),
+    ]
+    corner_seeds = [
+        send(pack_v.at[0, 3], hd_v.at[0, 0], (outer, above), *corner_above),
+        send(pack_v.at[1, 3], hd_v.at[0, 1], (partner, above), *to_above),
+        send(pack_v.at[0, 0], hd_v.at[1, 0], (outer, below), *corner_below),
+        send(pack_v.at[1, 0], hd_v.at[1, 1], (partner, below), *to_below),
+    ]
+    products = [
+        send(k_v.at[:, 4:6], hky_v.at[0], (gx, above), *to_above),
+        send(k_v.at[:, 0:2], hky_v.at[1], (gx, below), *to_below),
+        send(k_v.at[0], hkx_v.at[0], (outer, gy), *to_outer),
+        send(k_v.at[1], hkx_v.at[1], (partner, gy)),
+    ]
 
     applied = {}
     for y in (3, 0, 1, 2):
@@ -286,32 +318,12 @@
         applied[y] = total.astype(BF16)
     for y in (3, 0, 1, 2):
         relaxed = nt(applied[y], wb_v[y])
-        p0_v[y] = (st_v[y].astype(F32) - RELAX * relaxed).astype(BF16)
-    pl.semaphore_wait(barrier, awaited)
-    corner_above = (jnp.logical_and(has_outer, has_above), jnp.logical_and(has_outer, has_below))
-    corner_below = (corner_above[1], corner_above[0])
-    seeds = [
-        send(pack_v.at[:, 3], hy_v.at[0], (gx, above), *to_above),
-        send(pack_v.at[0, 3], hd_v.at[0, 0], (outer, above), *corner_above),
-        send(pack_v.at[1, 3], hd_v.at[0, 1], (partner, above), *to_above),
-        send(pack_v.at[:, 0], hy_v.at[1], (gx, below), *to_below),
-        send(pack_v.at[0, 0], hd_v.at[1, 0], (outer, below), *corner_below),
-        send(pack_v.at[1, 0], hd_v.at[1, 1], (partner, below), *to_below),
-        send(pack_v.at[0], hx_v.at[0], (outer, gy), *to_outer),
-        send(pack_v.at[1], hx_v.at[1], (partner, gy)),
-    ]
-    products = [
-        send(k_v.at[4:6], hky_v.at[0], (gx, above), *to_above),
-        send(k_v.at[0:2], hky_v.at[1], (gx, below), *to_below),
-        send(k_v.at[:, :, 0:128], hkx_v.at[:, :, 0:128], (outer, gy), *to_outer),
-        send(k_v.at[:, :, 128:256], hkx_v.at[:, :, 128:256], (partner, gy)),
-    ]
-
+        put_halves(p0_v, y, st_v[y].astype(F32) - RELAX * relaxed)
     first = [
-        send(p0_v.at[3], hp0y_v.at[0], (gx, above), *to_above),
-        send(p0_v.at[0], hp0y_v.at[1], (gx, below), *to_below),
-        send(p0_v.at[:, :, 0:128], hp0x_v.at[:, :, 0:128], (outer, gy), *to_outer),
-        send(p0_v.at[:, :, 128:256], hp0x_v.at[:, :, 128:256], (partner, gy)),
+        send(p0_v.at[:, 3], hp0y_v.at[0], (gx, above), *to_above),
+        send(p0_v.at[:, 0], hp0y_v.at[1], (gx, below), *to_below),
+        send(p0_v.at[0], hp0x_v.at[0], (outer, gy), *to_outer),
+        send(p0_v.at[1], hp0x_v.at[1], (partner, gy)),
     ]
 
     out[...] = jnp.zeros(out.shape, F32)
@@ -322,12 +334,10 @@
     halos, corners = {}, {}
     for end, y in ((1, 3), (0, 0)):
         halos[Y_AT[y]] = jnp.concatenate([hy_v[end, 0], hy_v[end, 1]], axis=1).astype(F32)
-        corners[y] = jnp.concatenate([hd_v[end, 0], hd_v[end, 1]], axis=1).astype(F32)
     for y in range(4):
         halos[X_AT[y]] = jnp.concatenate([hx_v[0, y], hx_v[1, y]], axis=1).astype(F32)
-    values = {at: slot_values(by_element(halos[at][0:MODES]), k_v[at]) for at in halos}
+    values = {at: slot_values(by_element(halos[at][0:MODES]), halves(k_v, at)) for at in halos}
     full = {at: spread_columns(values[at], halos[at][MODES:]) for at in halos}
-    corners_by = {y: by_element(corners[y][0:MODES]) for y in Y_AT}
     ly = {y: by_element(values[Y_AT[y]]) for y in Y_AT}
     for y in range(4):
         slot = full[X_AT[y]]
@@ -339,12 +349,12 @@
             lx_v[y, 128:192] = full[Y_AT[y]]
 
     def left(y, rows):
-        return jnp.concatenate([p0_v[y], lx_v[y, 0 : rows - 64]], axis=0)
+        return jnp.concatenate([halves(p0_v, y), lx_v[y, 0 : rows - 64]], axis=0)
 
     terms = [jnp.zeros((rows, 1), F32) for rows in (64, 64, 64, 32, 32)]
     for y in range(4):
         res = jnp.concatenate([res_v[0, y : y + 1, :], res_v[1, y : y + 1, :]], axis=1)
-        blocks = [(0, p0_v[y]), (1, lx_v[y, 0:64]), (2, lx_v[y, 64:128])]
+        blocks = [(0, halves(p0_v, y)), (1, lx_v[y, 0:64]), (2, lx_v[y, 64:128])]
         if y in Y_AT:
             blocks.append((3 if y == 0 else 4, ly[y]))
         for slot, block in blocks:
@@ -362,14 +372,18 @@
             size = 256 if y + 1 in Y_AT else 192
             acc_v[y, 0:size] = acc_v[y, 0:size] + nt(left(y + 1, size), w_v[y, 3])
 
+    await_all(corner_seeds)
+    for end, y in ((1, 3), (0, 0)):
+        corners[y] = jnp.concatenate([hd_v[end, 0], hd_v[end, 1]], axis=1).astype(F32)
+    corners_by = {y: by_element(corners[y][0:MODES]) for y in Y_AT}
     await_all(products)
     near_x, near_y, far_x, far_y = {}, {}, {}, {}
     for y in (3, 0, 1, 2):
-        near_x[y] = slot_values(seeds_by[y], hkx_v[X_AT[y]])
+        near_x[y] = slot_values(seeds_by[y], halves(hkx_v, X_AT[y]))
     for end, y in ((1, 3), (0, 0)):
-        near_y[y] = slot_values(seeds_by[y], hky_v[end, 1])
-        far_x[y] = slot_values(corners_by[y], hkx_v[Y_AT[y]])
-        far_y[y] = slot_values(corners_by[y], hky_v[end, 0])
+        near_y[y] = slot_values(seeds_by[y], halves(hky_v.at[end], 1))
+        far_x[y] = slot_values(corners_by[y], halves(hkx_v, Y_AT[y]))
+        far_y[y] = slot_values(corners_by[y], halves(hky_v.at[end], 0))
     near_x = {y: spread_columns(near_x[y], own[y][MODES:]) for y in range(4)}
     near_y = {y: spread_columns(near_y[y], own[y][MODES:]) for y in Y_AT}
     far_x = {y: spread_columns(far_x[y], corners[y][MODES:]) for y in Y_AT}
@@ -378,7 +392,7 @@
     await_all(first)
 
     def coupled(y):
-        rows = [hp0x_v[y], near_x[y]] + ([far_x[y]] if y in Y_AT else [])
+        rows = [halves(hp0x_v, y), near_x[y]] + ([far_x[y]] if y in Y_AT else [])
         part = nt(jnp.concatenate(rows, axis=0), w_v[y, 1])
         row_0 = acc_v[y, 0:64] + part[64:128]
         row_o, row_i, row_y = acc_v[y, 64:128], acc_v[y, 128:192], acc_v[y, 192:256]
@@ -389,7 +403,7 @@
             rows = [row_0.astype(BF16), row_y.astype(BF16), row_i, row_o]
             return jnp.concatenate(rows, axis=0)
         end = 0 if y == 0 else 1
-        rows = [hp0y_v[end], far_y[y], near_y[y]]
+        rows = [halves(hp0y_v, end, 1), far_y[y], near_y[y]]
         more = nt(jnp.concatenate(rows, axis=0), w_v[y, 2 + end])
         row_0, row_y = (row_0 + more[128:192]).astype(BF16), (row_y + more[0:64]).astype(BF16)
         corner = (part[128:192] + more[64:128]).astype(BF16)
@@ -508,6 +522,9 @@
             results.append(jnp.concatenate(rows, axis=0))
         return results
 
+    for copy, leaves in sends[: -len(msgs)]:
+        only(leaves, copy.wait_send)
+
     await_all(msgs[6:7])
     own_a, far_a = own_a + got(3), far_a + got(0)
     far_b, far_c = far_b + got(1), far_c + got(2)
@@ -518,6 +535,8 @@
     await_all(msgs[4:6])
     own_a, own_b, own_c = own_a + got(4), own_b + got(5), own_c + got(6)
     far_a = far_a + got(7)
+    for copy, leaves in sends[-len(msgs) :]:
+        only(leaves, copy.wait_send)
     await_all(msgs[0:2])
     (near_a, near_b), (past_a, past_b) = spread(0, 0), spread(0, 2)
     own_a, own_b = own_a + near_a, own_b + pick(near_b, 0.0)
@@ -547,9 +566,6 @@
         out[352:480] = b
         out[608:672] = c[64:128]
         out[800:801] = swap(a[96:97] + a[97:98])
-
-    for copy, leaves in sends:
-        only(leaves, copy.wait_send)
 
 
 def finish_kernel(data, coarse, restricted, row, sem):
@@ -582,12 +598,12 @@
         pltpu.VMEM((2, 4, 16, 128), BF16),
         pltpu.VMEM((2, 2, 16, 128), BF16),
         pltpu.VMEM((2, 2, 16, 128), BF16),
-        pltpu.VMEM((6, 64, 256), BF16),
-        pltpu.VMEM((6, 64, 256), BF16),
-        pltpu.VMEM((2, 2, 64, 256), BF16),
-        pltpu.VMEM((4, 64, 256), BF16),
-        pltpu.VMEM((4, 64, 256), BF16),
-        pltpu.VMEM((2, 64, 256), BF16),
+        pltpu.VMEM((2, 6, 64, 128), BF16),
+        pltpu.VMEM((2, 6, 64, 128), BF16),
+        pltpu.VMEM((2, 2, 2, 64, 128), BF16),
+        pltpu.VMEM((2, 4, 64, 128), BF16),
+        pltpu.VMEM((2, 4, 64, 128), BF16),
+        pltpu.VMEM((2, 2, 64, 128), BF16),
         pltpu.VMEM((4, 64, 256), BF16),
         pltpu.VMEM((4, 192, 256), BF16),
         pltpu.VMEM((4, 256, 256), F32),

time: 23.9 us -> 23.8 us (level)
  no operation moved by 1% of the time
where the time goes in v6:
time: 23.8 us; the launch traced here: 23.7 us
  Pallas kernels  23 us (97%)
  between operations  0.64 us (3%)
    pallas_call x1, Pallas kernels, body(): pl.pallas_call(call, out_shape=pltpu.VMEM((808, 128), F32), in_specs=[hbm...  22.3 us
    pallas_call x1, Pallas kernels, body(): pl.pallas_call(finish_kernel, out_shape=(jax.ShapeDtypeStruct((1, 1, 800,...  0.77 us

profile of v6, /device:TPU:30, one launch (start us, length us, event | category | flops | bytes accessed | tf_op | source)
XLA Modules:
  0.0 23.7 jit_solution(3526540023431155781)
XLA Ops:
  0.6 22.3 %galerkin.1.data = f32[808,128]{1,0:T(8,128)S(1)} custom-call(bf16[2,4,2,64,448]{4,3,2,1,0:T(8,128)(2,1)} %refs_0_.1, bf16[2,4,64,128]{3,2,1,0:T(8,128)(2,1)} %refs_1_.1, bf16[2,4,8,128]{3,2,1,0:T(8,128)(2,1)} %refs_2_.1, s32[2,2,4]{2,1,0:T(2,128)} %bitcast.2, f32[2,4,128]{2,1,0:T(4,128)} %refs_4_.1), custom_call_target="tpu_custom_call" | custom-call | tf_op jit(solution)/shard_map/galerkin/pallas_call | solution.py:623
  22.9 0.8 %store.1 = (f32[1,1,800,128]{3,2,1,0:T(8,128)}, f32[1,1,64]{2,1,0:T(1,128)}) custom-call(f32[808,128]{1,0:T(8,128)S(1)} %galerkin.1.data), custom_call_target="tpu_custom_call" | custom-call | tf_op jit(solution)/shard_map/store/pallas_call | solution.py:634

commit v7 on v5

--- a/solution.py
+++ b/solution.py
@@ -152,7 +152,7 @@
         big.append(load(inverse.at[x], inv_v.at[side]))
         big.append(load(residual.at[x], res_v.at[side]))
 
-    sends = []
+    sends, pending = [], []
 
     def send(src, dst, peer, leaves=None, arrives=None):
         at = len(sends)
@@ -164,13 +164,23 @@
             device_id=peer,
             device_id_type=MESH,
         )
-        only(leaves, copy.start)
         sends.append((copy, leaves))
+        pending.append((copy, leaves))
         return copy, arrives
 
+    def together(copies, act):
+        groups = {}
+        for copy, condition in copies:
+            groups.setdefault(id(condition), (condition, []))[1].append(copy)
+        for condition, group in groups.values():
+            only(condition, lambda group=group: [act(copy) for copy in group] and None)
+
+    def launch():
+        together(pending, lambda copy: copy.start())
+        pending.clear()
+
     def await_all(copies):
-        for copy, arrives in copies:
-            only(arrives, copy.wait_recv)
+        together(copies, lambda copy: copy.wait_recv())
 
     to_outer, to_outer2 = (has_outer, has_outer), (has_outer, has_back)
     to_below, to_above = (has_below, has_above), (has_above, has_below)
@@ -314,6 +324,7 @@
         send(p0_v.at[:, :, 128:256], hp0x_v.at[:, :, 128:256], (partner, gy)),
     ]
 
+    launch()
     out[...] = jnp.zeros(out.shape, F32)
     seeds_by = {y: by_element(own[y][0:MODES]) for y in range(4)}
     blank = jnp.zeros((64, 128), BF16)
@@ -448,6 +459,8 @@
             send(sny_v.at[end, 2:4], rcy_v.at[1 - end, 2:4], (partner, peer), *way),
         ]
 
+    launch()
+
     def summed(slot):
         a0, a1, a2 = tiles(g0, slot)
         b0, b1, b2 = tiles(g3, slot)
@@ -474,6 +487,7 @@
         send(snd_v.at[4:7], rcv_v.at[4:7], (outer, gy), *to_outer),
         send(snd_v.at[7:8], rcv_v.at[7:8], (outer2, gy), *to_outer2),
     ]
+    launch()
     um, up, mid, om, op, o_sum, im, ip, i_sum = summed(2)
     post(3, [with_terms(half(pick(by_side(ip, im), i_sum), False), terms[2])])
     far_a = half(pick(by_side(im, ip), i_sum), True)
@@ -489,6 +503,7 @@
         ],
     )
     msgs += [send(snd_v.at[0:4], rcv_v.at[0:4], (partner, gy))]
+    launch()
     own_a = with_terms(half(swap(pick(mid, by_side(um, up))), True), terms[0])
     own_b = swap(pick(op, o_sum))
     own_c = pick(om, 0.0)
@@ -548,8 +563,7 @@
         out[608:672] = c[64:128]
         out[800:801] = swap(a[96:97] + a[97:98])
 
-    for copy, leaves in sends:
-        only(leaves, copy.wait_send)
+    together(sends, lambda copy: copy.wait_send())
 
 
 def finish_kernel(data, coarse, restricted, row, sem):

time: 23.9 us -> 23.9 us (level)
  no operation moved by 1% of the time
where the time goes in v7:
time: 23.9 us; the launch traced here: 23.7 us
  Pallas kernels  23.1 us (97%)
  between operations  0.64 us (3%)
    pallas_call x1, Pallas kernels, body(): pl.pallas_call(call, out_shape=pltpu.VMEM((808, 128), F32), in_specs=[hbm...  22.3 us
    pallas_call x1, Pallas kernels, body(): pl.pallas_call(finish_kernel, out_shape=(jax.ShapeDtypeStruct((1, 1, 800,...  0.77 us

profile of v7, /device:TPU:30, one launch (start us, length us, event | category | flops | bytes accessed | tf_op | source)
XLA Modules:
  0.0 23.7 jit_solution(142537844500633758)
XLA Ops:
  0.6 22.3 %galerkin.1.data = f32[808,128]{1,0:T(8,128)S(1)} custom-call(bf16[2,4,2,64,448]{4,3,2,1,0:T(8,128)(2,1)} %refs_0_.1, bf16[2,4,64,128]{3,2,1,0:T(8,128)(2,1)} %refs_1_.1, bf16[2,4,8,128]{3,2,1,0:T(8,128)(2,1)} %refs_2_.1, s32[2,2,4]{2,1,0:T(2,128)} %bitcast.2, f32[2,4,128]{2,1,0:T(4,128)} %refs_4_.1), custom_call_target="tpu_custom_call" | custom-call | tf_op jit(solution)/shard_map/galerkin/pallas_call | solution.py:621
  22.9 0.8 %store.1 = (f32[1,1,800,128]{3,2,1,0:T(8,128)}, f32[1,1,64]{2,1,0:T(1,128)}) custom-call(f32[808,128]{1,0:T(8,128)S(1)} %galerkin.1.data), custom_call_target="tpu_custom_call" | custom-call | tf_op jit(solution)/shard_map/store/pallas_call | solution.py:632
